TPU v7x, 128 devices: a whole 4x4x4 slice. The times are simulated.
128 devices in a mesh: cols: 32 (over y, z, core), rows: 4 (over x).
Axes of the slice: x: 4, y: 4, z: 4, core: 2. Of those that a mesh axis runs over, the one named last changes fastest.
Arguments:
- observed: float32 [1024, 32768], P('rows', 'cols'), may hold values from -14 to 14
- class_map: int32 [1024, 32768], P('rows', 'cols'), may hold values from 0 to 3
- class_weights: float32 [4], replicated, may hold values from 0.5 to 8
- blur_kernel: float32 [3, 3], replicated, may hold values from 0.02 to 0.25
Outputs:
- solution: float32 [1024, 32768], P('rows', 'cols')
- residual: float32 [1024, 32768], P('rows', 'cols')
All inputs are finite; a program needn't handle non-finite values.
Results may differ from a plain program's by a relative error of at most 0.0003.
Values sent between devices are 32-bit elements; how exact they have to be, the bound alone decides.
A program may use at most 128 MiB of HBM per device.

v0:
```python
import jax
import jax.numpy as jnp
from jax import lax
from jax.sharding import PartitionSpec as P

COARSE = 8
SWEEPS = 8
ITERS = 2
CLASSES = 4


OMEGA = 0.8


def padded_2(cells, sides, width):
    for axis, dim in sides:
        count = lax.axis_size(axis)
        ends = count - 1
        head = lax.slice_in_dim(cells, 0, width, axis=dim)
        tail = lax.slice_in_dim(cells, cells.shape[dim] - width, cells.shape[dim], axis=dim)
        cells = jnp.concatenate(
            [
                lax.ppermute(tail, axis, [(i, (i + 1) % count) for i in range(ends)]),
                cells,
                lax.ppermute(head, axis, [((i + 1) % count, i) for i in range(ends)]),
            ],
            axis=dim,
        )
    return cells


def blurred(padded, kernel):
    height = padded.shape[0] - 2
    breadth = padded.shape[1] - 2
    summed = jnp.zeros((height, breadth), jnp.float32)
    for across in range(3):
        for along in range(3):
            summed = (
                summed
                + kernel[across, along] * padded[across : across + height, along : along + breadth]
            )
    return summed


def adjoint(padded, kernel):
    height = padded.shape[0] - 2
    breadth = padded.shape[1] - 2
    summed = jnp.zeros((height, breadth), jnp.float32)
    for across in range(3):
        for along in range(3):
            summed = (
                summed
                + kernel[across, along]
                * padded[2 - across : 2 - across + height, 2 - along : 2 - along + breadth]
            )
    return summed


def edge_weights(cond_pad):
    center = cond_pad[1:-1, 1:-1]
    return (
        0.5 * (center + cond_pad[1:-1, 2:]),
        0.5 * (center + cond_pad[1:-1, :-2]),
        0.5 * (center + cond_pad[:-2, 1:-1]),
        0.5 * (center + cond_pad[2:, 1:-1]),
    )


def laplace(padded, edge_set):
    east, west, north, south = edge_set
    center = padded[1:-1, 1:-1]
    return (
        (east + west + north + south) * center
        - east * padded[1:-1, 2:]
        - west * padded[1:-1, :-2]
        - north * padded[:-2, 1:-1]
        - south * padded[2:, 1:-1]
    )


def coarse_weights(edge_set, kernel):
    east, west, north, south = edge_set
    blocks_down = east.shape[0] // COARSE
    blocks_across = east.shape[1] // COARSE
    c_east = east[:, COARSE - 1 :: COARSE].reshape(blocks_down, COARSE, blocks_across).sum(axis=1)
    c_west = west[:, 0::COARSE].reshape(blocks_down, COARSE, blocks_across).sum(axis=1)
    c_north = north[0::COARSE, :].reshape(blocks_down, blocks_across, COARSE).sum(axis=2)
    c_south = south[COARSE - 1 :: COARSE, :].reshape(blocks_down, blocks_across, COARSE).sum(axis=2)
    c_diag = COARSE * COARSE * jnp.square(jnp.sum(kernel)) + c_east + c_west + c_north + c_south
    return jnp.stack([c_east, c_west, c_north, c_south, c_diag])


def jacobi(source, coarse_table, widen):
    c_east, c_west, c_north, c_south, c_diag = (
        coarse_table[0],
        coarse_table[1],
        coarse_table[2],
        coarse_table[3],
        coarse_table[4],
    )
    iterate = OMEGA * source / c_diag
    for repeat in range(SWEEPS - 1):
        padded = widen(iterate)
        applied = (
            c_diag * iterate
            - c_east * padded[1:-1, 2:]
            - c_west * padded[1:-1, :-2]
            - c_north * padded[:-2, 1:-1]
            - c_south * padded[2:, 1:-1]
        )
        iterate = iterate + OMEGA * (source - applied) / c_diag
    return iterate


def body(observed, class_map, class_weights, blur_kernel):
    rows_here = observed.shape[0]
    cols_here = observed.shape[1]
    conductance = jnp.zeros(observed.shape, jnp.float32)
    for class_id in range(CLASSES):
        conductance = conductance + jnp.where(class_map == class_id, class_weights[class_id], 0.0)
    rim_pair = padded_2(jnp.stack([observed, conductance]), (("cols", 2), ("rows", 1)), 1)
    edge_set = edge_weights(rim_pair[1])
    right_side = adjoint(rim_pair[0], blur_kernel)
    fine_diag = (
        jnp.sum(blur_kernel * blur_kernel) + edge_set[0] + edge_set[1] + edge_set[2] + edge_set[3]
    )
    coarse_table = coarse_weights(edge_set, blur_kernel)
    blocks_down = coarse_table.shape[1]
    blocks_across = coarse_table.shape[2]

    def widen_both(iterate):
        return padded_2(iterate, (("cols", 1), ("rows", 0)), 1)

    def coarse_part(source):
        return jacobi(source, coarse_table, widen_both)

    def precondition(residual):
        source = residual.reshape(blocks_down, COARSE, blocks_across, COARSE).sum(axis=(1, 3))
        coarse = coarse_part(source)
        spread = jnp.broadcast_to(
            coarse[:, None, :, None], (blocks_down, COARSE, blocks_across, COARSE)
        )
        return residual / fine_diag + spread.reshape(rows_here, cols_here)

    solution = jnp.zeros(observed.shape, jnp.float32)
    residual = right_side

    def measure(first, second):
        return lax.psum(jnp.sum(first * second), ("cols", "rows"))

    precond = precondition(residual)
    gamma_now = measure(residual, precond)
    direction = precond
    for iteration in range(ITERS):
        padded = padded_2(direction, (("cols", 1), ("rows", 0)), 1)
        image = blurred(padded, blur_kernel)
        blurred_rim = padded_2(image, (("cols", 1), ("rows", 0)), 1)
        product_field = adjoint(blurred_rim, blur_kernel) + laplace(padded, edge_set)
        step_size = gamma_now / lax.psum(jnp.sum(direction * product_field), ("cols", "rows"))
        solution = solution + step_size * direction
        residual = residual - step_size * product_field
        if iteration + 1 < ITERS:
            precond = precondition(residual)
            gamma_next = measure(residual, precond)
            direction = precond + gamma_next / gamma_now * direction
            gamma_now = gamma_next
    return (solution, residual)


def solution(mesh):
    return jax.shard_map(
        body,
        mesh=mesh,
        in_specs=(P("rows", "cols"), P("rows", "cols"), P(), P()),
        out_specs=(P("rows", "cols"), P("rows", "cols")),
        check_vma=False,
    )
```

profile of v0, /device:TPU:1, one launch (start us, length us, event | category | flops | bytes accessed | tf_op | source)
XLA Modules:
  0.0 756.3 jit_solution(9630674649115675300)
XLA Ops:
  35.3 6.1 slice.757
  48.7 7.4 fusion.78
  56.1 11.3 %reshape.30 = f32[32,8,128,8]{3,2,1,0:T(8,128)} reshape(f32[256,1024]{1,0:T(8,128)S(1)} %fusion.78) | data formatting | bytes 2097152 | tf_op jit(solution)/shard_map/reshape | solution.py:138
  68.4 7.0 reduce_sum.109
  75.4 5.8 collective-permute-start.5
  125.0 5.4 collective-permute-start.17
  142.0 5.1 collective-permute-start.21
  192.6 8.0 %broadcast_in_dim.37 = f32[32,8,128,8]{3,2,1,0:T(8,128)} broadcast(f32[32,128]{1,0:T(8,128)S(1)} %fusion.177), dimensions={0,2} | broadcast | bytes 1064960 | tf_op jit(solution)/shard_map/broadcast_in_dim | solution.py:140
  200.7 13.5 %reshape.35 = f32[256,1024]{1,0:T(8,128)} reshape(f32[32,8,128,8]{3,2,1,0:T(8,128)} %broadcast_in_dim.37) | data formatting | bytes 2097152 | tf_op jit(solution)/shard_map/reshape | solution.py:143
  214.1 11.1 %divide_add_fusion.1 = (f32[256,1024]{1,0:T(8,128)S(1)}, f32[256,1024]{1,0:T(8,128)}) fusion(f32[256,1024]{1,0:T(8,128)} %reshape.35, f32[256,1024]{1,0:T(8,128)} %get-tuple-element.22, f32[256,1024]{1,0:T(8,128)} %copy-done.1, f32[256,1024]{1,0:T(8,128)} %get-tuple-element.21, f32[256,1024]{1,0:T(8,128)S(1)} %get-tuple-element.19, f32[]{:T(128)} %get-tuple-element.4, ...), kind=kLoop, calls=%fused_computation.165 | loop fusion | flops 6029312 | bytes 16777256 | tf_op jit(solution)/shard_map/add | solution.py:143
  242.7 11.5 %fusion.53 = f32[256,1024]{1,0:T(8,128)S(1)} fusion(f32[256,1026]{1,0:T(8,128)} %concatenate.347, f32[1,1026]{1,0:T(1,128)S(1)} %collective-permute-done.35, f32[1,1026]{1,0:T(1,128)S(1)} %collective-permute-done.34, f32[256,1024]{1,0:T(8,128)S(1)} %get-tuple-element.11, f32[256,1]{1,0:T(8,128)} %collective-permute-done.32, ...), kind=kLoop, calls=%fused_computation.93 | loop fusion | flops 6553600 | bytes 3158068 | tf_op jit(solution)/shard_map/add | solution.py:39
  257.2 5.9 collective-permute-start.36
  274.2 19.3 %multiply_reduce_fusion.2 = (f32[]{:T(128)}, f32[]{:T(128)}, f32[256,1024]{1,0:T(8,128)}) fusion(f32[256,1024]{1,0:T(8,128)S(1)} %get-tuple-element.11, f32[256,1024]{1,0:T(8,128)} %get-tuple-element.22, f32[1,1026]{1,0:T(1,128)S(1)} %collective-permute-done.35, f32[256,1026]{1,0:T(8,128)} %concatenate.347, f32[256,1024]{1,0:T(8,128)} %copy-done.1, ...), kind=kLoop, calls=%fused_computation.162 | loop fusion | flops 16515070 | bytes 18899020 | tf_op jit(solution)/shard_map/reduce_sum | solution.py:159
  293.5 82.9 %all-reduce = (f32[]{:T(128)}, f32[]{:T(128)}) all-reduce(f32[]{:T(128)} %get-tuple-element.3, f32[]{:T(128)} %get-tuple-element.2), channel_id=1, replica_groups=mesh['cols'=32,'rows'=4] {'cols','rows'}, use_global_device_ids=true, to_apply=%region_8.9 | all-reduce | flops 2 | bytes 16 | tf_op jit(solution)/shard_map/psum | solution.py:149
  377.5 8.6 %multiply_subtract_fusion.1 = f32[256,1024]{1,0:T(8,128)S(1)} fusion(f32[256,1024]{1,0:T(8,128)} %get-tuple-element.10, f32[]{:T(128)S(6)} %div.72, f32[258,1026]{1,0:T(8,128)S(1)} %get-tuple-element.13, f32[]{:T(128)} %bitcast.15, f32[]{:T(128)} %bitcast.14, f32[]{:T(128)} %bitcast.13, f32[]{:T(128)} %bitcast.12, f32[]{:T(128)} %bitcast.11, f32[]{:T(128)} %bitcast.10, ...), kind=kLoop, calls=%fused_computation.161 | loop fusion | flops 4980736 | bytes 11534376 | tf_op jit(solution)/shard_map/sub | solution.py:161
  386.1 11.3 %reshape.36 = f32[32,8,128,8]{3,2,1,0:T(8,128)} reshape(f32[256,1024]{1,0:T(8,128)S(1)} %multiply_subtract_fusion.1) | data formatting | bytes 2097152 | tf_op jit(solution)/shard_map/reshape | solution.py:138
  397.4 6.9 reduce_sum.117
  513.4 8.0 %broadcast_in_dim.38 = f32[32,8,128,8]{3,2,1,0:T(8,128)} broadcast(f32[32,128]{1,0:T(8,128)S(1)} %fusion.93), dimensions={0,2} | broadcast | bytes 1064960 | tf_op jit(solution)/shard_map/broadcast_in_dim | solution.py:140
  521.5 13.6 %reshape.37 = f32[256,1024]{1,0:T(8,128)} reshape(f32[32,8,128,8]{3,2,1,0:T(8,128)} %broadcast_in_dim.38) | data formatting | bytes 2097152 | tf_op jit(solution)/shard_map/reshape | solution.py:143
  537.3 74.7 %psum.30 = f32[]{:T(128)} all-reduce(f32[]{:T(128)} %multiply_reduce_fusion.1), channel_id=1, replica_groups=mesh['cols'=32,'rows'=4] {'cols','rows'}, use_global_device_ids=true, to_apply=%region_13.14 | all-reduce | flops 1 | bytes 8 | tf_op jit(solution)/shard_map/psum | solution.py:149
  631.1 11.4 %fusion.22 = f32[256,1024]{1,0:T(8,128)S(1)} fusion(f32[256,1026]{1,0:T(8,128)} %concatenate.392, f32[1,1026]{1,0:T(1,128)S(1)} %collective-permute-done.71, f32[1,1026]{1,0:T(1,128)S(1)} %collective-permute-done.70, f32[256,1024]{1,0:T(8,128)S(1)} %multiply_add_fusion.1, f32[256,1]{1,0:T(8,128)S(1)} %collective-permute-done.68, ...), kind=kLoop, calls=%fused_computation.62 | loop fusion | flops 6553600 | bytes 3158068 | tf_op jit(solution)/shard_map/add | solution.py:39
  645.5 5.8 collective-permute-start.72
  662.3 18.0 %multiply_reduce_fusion = (f32[]{:T(128)}, f32[256,1024]{1,0:T(8,128)}) fusion(f32[256,1024]{1,0:T(8,128)S(1)} %multiply_add_fusion.1, f32[256,1024]{1,0:T(8,128)} %get-tuple-element.22, f32[1,1026]{1,0:T(1,128)S(1)} %collective-permute-done.71, f32[256,1026]{1,0:T(8,128)} %concatenate.392, f32[256,1024]{1,0:T(8,128)} %copy-done.1, ...), kind=kLoop, calls=%fused_computation.157 | loop fusion | flops 11534335 | bytes 9461832 | tf_op jit(solution)/shard_map/reduce_sum | solution.py:159
  680.4 71.6 %psum.31 = f32[]{:T(128)} all-reduce(f32[]{:T(128)} %get-tuple-element.8), channel_id=1, replica_groups=mesh['cols'=32,'rows'=4] {'cols','rows'}, use_global_device_ids=true, to_apply=%region_15.16 | all-reduce | flops 1 | bytes 8 | tf_op jit(solution)/shard_map/psum | solution.py:159
  (246 shorter events, 319.1 us)
Async XLA Ops:
  6.4 9.0 %collective-permute-start.1 = (f32[2,256,1]{2,1,0:T(8,128)S(1)}, f32[2,256,1]{2,1,0:T(8,128)S(1)}, u32[]{:S(2)}, u32[]{:S(2)}) collective-permute-start(f32[2,256,1]{2,1,0:T(8,128)S(1)} %get-tuple-element.17), channel_id=1, source_target_pairs={{4,0},{8,4},{12,8},{16,12},{20,16},{24,20},{28,24},{32,28},{36,32}... | collective-permute-start | bytes 6152 | tf_op jit(solution)/shard_map/ppermute | solution.py:25
  9.8 6.8 collective-permute-start
  19.7 6.4 collective-permute-start.2
  75.4 7.8 %collective-permute-start.5 = (f32[32,1]{1,0:T(8,128)S(1)}, f32[32,1]{1,0:T(8,128)S(1)}, u32[]{:S(2)}, u32[]{:S(2)}) collective-permute-start(f32[32,1]{1,0:T(8,128)S(1)} %get-tuple-element.93), channel_id=1, source_target_pairs={{0,4},{4,8},{8,12},{12,16},{16,20},{20,24},{24,28},{28,32},{32,36}... | collective-permute-start | bytes 392 | tf_op jit(solution)/shard_map/ppermute | solution.py:23
  94.0 5.3 collective-permute-start.9
  125.0 7.3 collective-permute-start.17
  142.0 7.1 collective-permute-start.21
  147.1 5.4 collective-permute-start.20
  159.0 6.8 collective-permute-start.25
  163.8 5.7 collective-permute-start.24
  176.0 6.5 collective-permute-start.29
  180.6 5.7 collective-permute-start.28
  225.3 7.2 collective-permute-start.33
  227.3 6.5 collective-permute-start.32
  255.3 8.6 %collective-permute-start.37 = (f32[256,1]{1,0:T(8,128)S(1)}, f32[256,1]{1,0:T(8,128)}, u32[]{:S(2)}, u32[]{:S(2)}) collective-permute-start(f32[256,1]{1,0:T(8,128)S(1)} %get-tuple-element.35), channel_id=1, source_target_pairs={{4,0},{8,4},{12,8},{16,12},{20,16},{24,20},{28,24},{32,28},{36,32}... | collective-permute-start | bytes 3080 | tf_op jit(solution)/shard_map/ppermute | solution.py:25
  257.2 7.8 %collective-permute-start.36 = (f32[256,1]{1,0:T(8,128)S(1)}, f32[256,1]{1,0:T(8,128)}, u32[]{:S(2)}, u32[]{:S(2)}) collective-permute-start(f32[256,1]{1,0:T(8,128)S(1)} %get-tuple-element.36), channel_id=1, source_target_pairs={{0,4},{4,8},{8,12},{12,16},{16,20},{20,24},{24,28},{28,32},{32,36}... | collective-permute-start | bytes 3080 | tf_op jit(solution)/shard_map/ppermute | solution.py:23
  268.2 5.5 collective-permute-start.38
  480.1 6.4 collective-permute-start.61
  484.6 5.7 collective-permute-start.60
  496.8 6.5 collective-permute-start.65
  501.4 5.7 collective-permute-start.64
  615.3 6.3 collective-permute-start.69
  643.5 8.5 %collective-permute-start.73 = (f32[256,1]{1,0:T(8,128)S(1)}, f32[256,1]{1,0:T(8,128)}, u32[]{:S(2)}, u32[]{:S(2)}) collective-permute-start(f32[256,1]{1,0:T(8,128)S(1)} %get-tuple-element.31), channel_id=1, source_target_pairs={{4,0},{8,4},{12,8},{16,12},{20,16},{24,20},{28,24},{32,28},{36,32}... | collective-permute-start | bytes 3080 | tf_op jit(solution)/shard_map/ppermute | solution.py:25
  645.5 7.7 %collective-permute-start.72 = (f32[256,1]{1,0:T(8,128)S(1)}, f32[256,1]{1,0:T(8,128)}, u32[]{:S(2)}, u32[]{:S(2)}) collective-permute-start(f32[256,1]{1,0:T(8,128)S(1)} %get-tuple-element.32), channel_id=1, source_target_pairs={{0,4},{4,8},{8,12},{12,16},{16,20},{20,24},{24,28},{28,32},{32,36}... | collective-permute-start | bytes 3080 | tf_op jit(solution)/shard_map/ppermute | solution.py:23
  (61 other events, 526.1 us)
where the time goes:
time: 769 us; the launch traced here: 756 us
  blocking collectives  229 us (30%)
  starting transfers between devices  190 us (25%)
  other arithmetic  123 us (16%)
  waiting for transfers between devices  106 us (14%)
  local copies, waits for them, and re-layouts  102 us (13%)
    psum x2, blocking collectives, measure(): return lax.psum(jnp.sum(first * second), ('cols', 'rows'))  158 us
    ppermute x38, starting transfers between devices, padded_2(): lax.ppermute(tail, axis, [(i, (i + 1) % count) for i in range(ends)])  125 us
    ppermute x38, waiting for transfers between devices, padded_2(): lax.ppermute(head, axis, [((i + 1) % count, i) for i in range(ends)])  98.4 us
    psum x1, blocking collectives, body(): lax.psum(jnp.sum(direction * product_field), ('cols', 'rows'))  71.6 us
    ppermute x38, starting transfers between devices, padded_2(): lax.ppermute(head, axis, [((i + 1) % count, i) for i in range(ends)])  64.4 us
    reduce_sum x2, other arithmetic, body(): jnp.sum(direction * product_field)  37.3 us
    reshape x2, local copies, waits for them, and re-layouts, precondition(): return residual / fine_diag + spread.reshape(rows_here, cols_here)  27 us
    add x2, other arithmetic, blurred(): summed + kernel[across, along] * padded[across:across + height, along:alo...  22.8 us
  transfers between devices with their start and end apart: 76, of which 42 were waited for; matrix products, arithmetic and copies ran while one was open for 0% of the time, Pallas kernels for 0%

commit v1 on v0

v1 whole, which is shorter than its diff:
```python
import functools

import jax
import jax.numpy as jnp
from jax import lax
from jax.experimental import pallas as pl
from jax.experimental.pallas import tpu as pltpu
from jax.sharding import PartitionSpec as P

MESH = pl.DeviceIdType.MESH
OMEGA = 0.8
SWEEPS = 8
NB = ((-1, 0), (1, 0), (0, -1), (0, 1), (-1, -1), (-1, 1), (1, -1), (1, 1))
F32 = jnp.float32
BF16 = jnp.bfloat16


def split2(x):
    hi = x.astype(BF16)
    lo = (x - hi.astype(F32)).astype(BF16)
    return hi, lo


def kernel(
    n_rows, n_cols, zk,
    cw, bk, obs_hbm, cls_hbm, sol_hbm, res_hbm,
    obs, cls, cond, r0, rfd, ce, cs, d0, img, q0, w, lw, sol, res,
    zup, cmat, umat, tbuf, tt0, tt1, tt2, hbuf, ctab, zs,
    sn0, ss0, rn0, rs0, rx0, sn1, rn1, rs1, rx1, sn2, ss2, rn2, rs2, rx2,
    red0, red1, redx, redy,
    in_sem, out_sem, send_sem, recv_sem, rsend, rrecv,
):
    r = lax.axis_index("rows")
    c = lax.axis_index("cols")
    ny = n_cols // zk
    y, k8 = c // zk, lax.rem(c, zk)

    def ok(dr, dc):
        return (r + dr >= 0) & (r + dr < n_rows) & (c + dc >= 0) & (c + dc < n_cols)

    def dev(dr, dc):
        return (c + dc, r + dr)

    loads = []
    for t in range(8):
        lanes = pl.ds(t * 128, 128)
        loads.append(pltpu.make_async_copy(cls_hbm.at[:, lanes], cls.at[t], in_sem.at[t]))
        loads.append(pltpu.make_async_copy(
            obs_hbm.at[:, lanes], obs.at[t, pl.ds(16, 256), :], in_sem.at[8 + t]))
    for x in loads:
        x.start()

    for buf in (rn0, rs0, rx0, rn1, rs1, rx1, rn2, rs2, rx2, hbuf, zs):
        buf[...] = jnp.zeros(buf.shape, F32)

    bar = pltpu.get_barrier_semaphore()
    peers = zk + n_rows * ny - 2
    for dr, dc in NB:
        if dc == 0:
            continue
        fresh = ok(dr, dc)
        if dr == 0:
            fresh = fresh & (k8 == (zk - 1 if dc > 0 else 0))
        peers = peers + fresh.astype(jnp.int32)

        @pl.when(fresh)
        def _():
            pl.semaphore_signal(bar, inc=1, device_id=dev(dr, dc), device_id_type=MESH)
    zk_group = [(y * zk + i, r) for i in range(zk)]
    xy_me = r * ny + y
    xy_group = [(j * zk + k8, i) for i in range(n_rows) for j in range(ny)]
    for i in range(zk):
        @pl.when(k8 != i)
        def _():
            pl.semaphore_signal(bar, inc=1, device_id=zk_group[i], device_id_type=MESH)
    for i in range(n_rows * ny):
        @pl.when(xy_me != i)
        def _():
            pl.semaphore_signal(bar, inc=1, device_id=xy_group[i], device_id_type=MESH)

    lane = lax.broadcasted_iota(jnp.int32, (8, 128), 1)
    sub = lax.broadcasted_iota(jnp.int32, (8, 128), 0)
    first_lane = lane == 0
    last_lane = lane == 127

    ii = lax.broadcasted_iota(jnp.int32, (1024, 128), 0)
    jj = lax.broadcasted_iota(jnp.int32, (1024, 128), 1)
    cmat[:, 0:128] = jnp.where(ii // 8 == jj, 1.0, 0.0).astype(BF16)
    cmat[:, 128:256] = jnp.where(ii == jj * 8 + 7, 1.0, 0.0).astype(BF16)
    ui = lax.broadcasted_iota(jnp.int32, (128, 1024), 0)
    uj = lax.broadcasted_iota(jnp.int32, (128, 1024), 1)
    umat[:, 0:1024] = jnp.where(uj // 8 == ui, 1.0, 0.0).astype(BF16)
    vi = lax.broadcasted_iota(jnp.int32, (128, 128), 0)
    vj = lax.broadcasted_iota(jnp.int32, (128, 128), 1)
    umat[:, 1024:1152] = jnp.where(
        ((vj < 64) & (vi == 0)) | ((vj >= 64) & (vi == 127)), 1.0, 0.0).astype(BF16)

    kk = [[bk[a * 3 + b] for b in range(3)] for a in range(3)]
    ksum = kk[0][0]
    ksq = kk[0][0] * kk[0][0]
    for a in range(3):
        for b in range(3):
            if a + b:
                ksum = ksum + kk[a][b]
                ksq = ksq + kk[a][b] * kk[a][b]

    def sh_east(v):
        rolled = [pltpu.roll(x, 127, 1) for x in v]
        n = len(v)
        return [jnp.where(last_lane, rolled[(t + 1) % n], rolled[t]) for t in range(n)]

    def sh_west(v):
        rolled = [pltpu.roll(x, 1, 1) for x in v]
        n = len(v)
        return [jnp.where(first_lane, rolled[(t - 1) % n], rolled[t]) for t in range(n)]

    def rows_of(ref, base, n=9):
        return [ref[t, pl.ds(base, 8), :] for t in range(n)]

    for x in loads:
        x.wait()

    w0, w1, w2, w3 = cw[0], cw[1], cw[2], cw[3]

    def cond_body(i, _):
        src = pl.multiple_of(i * 8, 8)
        dst = pl.multiple_of(i * 8 + 16, 8)
        for t in range(8):
            m = cls[t, pl.ds(src, 8), :]
            cond[t, pl.ds(dst, 8), :] = jnp.where(
                m == 0, w0, jnp.where(m == 1, w1, jnp.where(m == 2, w2, w3)))
        return 0

    lax.fori_loop(0, 32, cond_body, 0)

    for t in range(8):
        sn0[t] = jnp.where(sub < 4, obs[t, 16:24, :], pltpu.roll(cond[t, 16:24, :], 4, 0))
        ss0[t] = jnp.where(sub >= 4, obs[t, 264:272, :], pltpu.roll(cond[t, 264:272, :], 4, 0))

    def rim_tile(start, n):
        lanes = lax.broadcasted_iota(jnp.int32, (n, 128), 1)
        rows = pl.ds(start, n)
        left = jnp.where(lanes < 4, obs[0, rows, :], pltpu.roll(cond[0, rows, :], 4, 1))
        right = jnp.where(lanes >= 124, obs[7, rows, :], pltpu.roll(cond[7, rows, :], 124, 1))
        return jnp.where(lanes < 64, left, right)

    tt0[0] = rim_tile(16, 128).T
    tt0[1] = rim_tile(144, 128).T
    tbuf[...] = jnp.zeros(tbuf.shape, F32)
    tbuf[64:72, :] = rim_tile(264, 8)
    tbuf[72:80, :] = rim_tile(16, 8)
    tt0[2] = tbuf[...].T

    def side_copies(tt, rx, groups_diag):
        low, high = pl.ds(0, 8), pl.ds(120, 8)
        out = []
        for n, (dr, dc) in enumerate(NB):
            if dc == 0:
                continue
            groups = pl.ds(0, 3) if dr == 0 else groups_diag
            rows = low if dc < 0 else high
            out.append((n, tt.at[groups, rows, :], rx.at[n, groups]))
        return out

    def start_all(phase, copies):
        for n, src, dst in copies:
            dr, dc = NB[n]
            @pl.when(ok(dr, dc))
            def _():
                pltpu.make_async_remote_copy(
                    src, dst, send_sem.at[phase, n], recv_sem.at[phase, n],
                    device_id=dev(dr, dc), device_id_type=MESH).start()

    def wait_recv_all(phase, copies):
        for n, src, dst in copies:
            dr, dc = NB[n]
            @pl.when(ok(-dr, -dc))
            def _():
                pltpu.make_async_remote_copy(
                    src, dst, send_sem.at[phase, n], recv_sem.at[phase, n],
                    device_id=dev(-dr, -dc), device_id_type=MESH).wait_recv()

    def wait_send_all(phase, copies):
        for n, src, dst in copies:
            dr, dc = NB[n]
            @pl.when(ok(dr, dc))
            def _():
                pltpu.make_async_remote_copy(
                    src, dst, send_sem.at[phase, n], recv_sem.at[phase, n],
                    device_id=dev(dr, dc), device_id_type=MESH).wait_send()

    third = pl.ds(2, 1)
    copies0 = [(0, sn0, rs0), (1, ss0, rn0)] + side_copies(tt0, rx0, third)

    pl.semaphore_wait(bar, peers)

    start_all(0, copies0)
    wait_recv_all(0, copies0)

    def side(rx, group, dc, in_north, in_center):
        north = rx[NB.index((1, dc)), group]
        center = rx[NB.index((0, dc)), group]
        south = rx[NB.index((-1, dc)), group]
        return jnp.where(in_north, north, jnp.where(in_center, center, south))

    fine_north = (lane < 8) | ((lane >= 64) & (lane < 72))
    fine_center = (lane >= 8) & (lane < 40)
    lane64 = lax.rem(lane, 64)

    def unpack_fine(rx):
        for dc, rows in ((-1, slice(0, 8)), (1, slice(120, 128))):
            here = NB.index((0, dc))
            hbuf[0, rows, :] = rx[here, 0]
            hbuf[1, rows, :] = rx[here, 1]
            hbuf[2, rows, :] = side(rx, 2, dc, fine_north, fine_center)

    unpack_fine(rx0)

    def cond_of(x):
        lanes = lax.broadcasted_iota(jnp.int32, x.shape, 1)
        return jnp.where(lanes < 64, pltpu.roll(x, 124, 1), pltpu.roll(x, 4, 1))

    for g in range(2):
        tile = hbuf[g].T
        rows = slice(16 + 128 * g, 144 + 128 * g)
        obs[8, rows, :] = tile
        cond[8, rows, :] = cond_of(tile)
    tile = hbuf[2].T
    for rows, lo in ((slice(8, 16), 64), (slice(272, 280), 72)):
        obs[8, rows, :] = tile[lo:lo + 8]
        cond[8, rows, :] = cond_of(tile[lo:lo + 8])
    for t in range(8):
        obs[t, 8:16, :] = rn0[t]
        cond[t, 8:16, :] = pltpu.roll(rn0[t], 4, 0)
        obs[t, 272:280, :] = rs0[t]
        cond[t, 272:280, :] = pltpu.roll(rs0[t], 4, 0)

    def fine_body(i, _):
        base = pl.multiple_of(i * 8 + 8, 8)
        up, mid, down = rows_of(obs, base - 1), rows_of(obs, base), rows_of(obs, base + 1)
        v = [[kk[0][b] * down[t] + kk[1][b] * mid[t] + kk[2][b] * up[t] for t in range(9)]
             for b in range(3)]
        e0, w2_ = sh_east(v[0]), sh_west(v[2])
        for t in range(9):
            r0[t, pl.ds(base, 8), :] = v[1][t] + e0[t] + w2_[t]
        return 0

    lax.fori_loop(0, 34, fine_body, 0)

    def edge_body(i, _):
        base = pl.multiple_of(i * 8 + 8, 8)
        north, mid, south = rows_of(cond, base - 1), rows_of(cond, base), rows_of(cond, base + 1)
        east, west = sh_east(mid), sh_west(mid)
        for t in range(9):
            here = pl.ds(base, 8)
            total = (east[t] + west[t]) + (north[t] + south[t])
            rfd[t, here, :] = 1.0 / (ksq + 2.0 * mid[t] + 0.5 * total)
            ce[t, here, :] = 0.5 * (mid[t] + east[t])
            cs[t, here, :] = 0.5 * (mid[t] + south[t])
        return 0

    lax.fori_loop(0, 34, edge_body, 0)

    def clear_outside(ref):
        @pl.when(r == 0)
        def _():
            for t in range(9):
                ref[t, 8:16, :] = jnp.zeros((8, 128), F32)

        @pl.when(r == n_rows - 1)
        def _():
            for t in range(9):
                ref[t, 272:280, :] = jnp.zeros((8, 128), F32)

        lanes = lax.broadcasted_iota(jnp.int32, (272, 128), 1)

        @pl.when(c == 0)
        def _():
            ref[8, 8:280, :] = jnp.where(lanes < 64, ref[8, 8:280, :], 0.0)

        @pl.when(c == n_cols - 1)
        def _():
            ref[8, 8:280, :] = jnp.where(lanes >= 64, ref[8, 8:280, :], 0.0)

    clear_outside(rfd)

    def row_sums(ref, t):
        total = ref[t, pl.ds(16, 32, stride=8), :]
        for s in range(1, 8):
            total = total + ref[t, pl.ds(16 + s, 32, stride=8), :]
        return total

    src = jnp.concatenate([row_sums(r0, t) for t in range(8)], axis=1)
    esum = jnp.concatenate([row_sums(ce, t) for t in range(8)], axis=1)
    srow = jnp.concatenate([cs[t, pl.ds(23, 32, stride=8), :] for t in range(8)], axis=1)
    nrow = jnp.concatenate([cs[t, 8:16, :] for t in range(8)], axis=1)
    stack = jnp.concatenate([src, esum, srow, nrow], axis=0)
    hi, lo = split2(stack)
    sums = jnp.dot(hi, cmat[...], preferred_element_type=F32) + jnp.dot(
        lo, cmat[...], preferred_element_type=F32)
    source = sums[0:32, 0:128]
    c_east = sums[32:64, 128:256]
    c_south = sums[64:96, 0:128]
    outer = row_sums(ce, 8)
    lane32 = lax.broadcasted_iota(jnp.int32, (32, 128), 1)
    c_west = jnp.where(lane32 == 0, pltpu.roll(outer, 1, 1), pltpu.roll(c_east, 1, 1))
    zs[0, 0:8, :] = sums[96:104, 0:128]
    zs[0, 8:40, :] = c_south
    c_north = zs[0, 7:39, :]
    zs[...] = jnp.zeros(zs.shape, F32)
    c_diag = 64.0 * (ksum * ksum) + c_east + c_west + c_north + c_south
    scale = OMEGA / c_diag
    fields = (source * scale, c_east * scale, c_west * scale, c_north * scale, c_south * scale)
    ctab[5, 0, 8:40, :] = scale
    for f in range(5):
        ctab[f, 0, 8:40, :] = fields[f]
        sn1[f] = fields[f]
    for g in range(3):
        for h in range(2):
            f = 2 * g + h
            if f < 5:
                tbuf[64 * h:64 * h + 8, :] = fields[f][24:32]
                tbuf[64 * h + 8:64 * h + 40, :] = fields[f]
                tbuf[64 * h + 40:64 * h + 48, :] = fields[f][0:8]
        tt1[g] = tbuf[...].T

    whole = pl.ds(0, 3)
    copies1 = [(0, sn1.at[:, pl.ds(0, 8), :], rs1), (1, sn1.at[:, pl.ds(24, 8), :], rn1)]
    copies1 += side_copies(tt1, rx1, whole)
    start_all(1, copies1)
    wait_recv_all(1, copies1)

    for f in range(5):
        ctab[f, 0, 0:8, :] = rn1[f]
        ctab[f, 0, 40:48, :] = rs1[f]
    for g in range(3):
        for dc, rows in ((-1, slice(0, 8)), (1, slice(120, 128))):
            hbuf[g, rows, :] = side(rx1, g, dc, lane64 < 8, lane64 < 40)
        tile = hbuf[g].T
        for h in range(2):
            f = 2 * g + h
            if f < 5:
                ctab[f, 1, :, :] = tile[64 * h:64 * h + 48]

    lane48 = lax.broadcasted_iota(jnp.int32, (48, 128), 1)
    last48, first48 = lane48 == 127, lane48 == 0

    def sweep(_, carry):
        z = [zs[t, 8:56, :] for t in range(2)]
        east = [pltpu.roll(x, 127, 1) for x in z]
        west = [pltpu.roll(x, 1, 1) for x in z]
        new = []
        for t in range(2):
            ze = jnp.where(last48, east[1 - t], east[t])
            zw = jnp.where(first48, west[1 - t], west[t])
            zn, zso = zs[t, 7:55, :], zs[t, 9:57, :]
            new.append((ctab[0, t] + (1.0 - OMEGA) * z[t])
                       + (ctab[1, t] * ze + ctab[2, t] * zw)
                       + (ctab[3, t] * zn + ctab[4, t] * zso))
        for t in range(2):
            zs[t, 8:56, :] = new[t]
        return carry

    def jacobi():
        for t in range(2):
            zs[t, 8:56, :] = ctab[0, t]
        lax.fori_loop(0, SWEEPS - 1, sweep, 0)
        hi0, lo0 = split2(zs[0, 8:56, :])
        hi1, lo1 = split2(zs[1, 8:56, :])
        up = jnp.dot(hi0, umat[:, 0:1024], preferred_element_type=F32) + jnp.dot(
            lo0, umat[:, 0:1024], preferred_element_type=F32)
        for t in range(8):
            zup[t] = up[:, 128 * t:128 * t + 128]
        zup[8] = jnp.dot(hi1, umat[:, 1024:1152], preferred_element_type=F32) + jnp.dot(
            lo1, umat[:, 1024:1152], preferred_element_type=F32)

    jacobi()

    def precond(field, out):
        def body(i, _):
            base = pl.multiple_of(i * 8 + 8, 8)
            here = pl.ds(base, 8)
            for t in range(9):
                out[t, here, :] = field[t, here, :] * rfd[t, here, :] + zup[t, pl.ds(i + 7, 1), :]
            return 0

        lax.fori_loop(0, 34, body, 0)

    precond(r0, d0)

    def blur_rows(ref, base):
        up, mid, down = rows_of(ref, base - 1), rows_of(ref, base), rows_of(ref, base + 1)
        u = [[kk[0][b] * up[t] + kk[1][b] * mid[t] + kk[2][b] * down[t] for t in range(9)]
             for b in range(3)]
        w_, e_ = sh_west(u[0]), sh_east(u[2])
        return [u[1][t] + w_[t] + e_[t] for t in range(9)], up, mid, down

    def blur0(i, _):
        base = pl.multiple_of(i * 8 + 8, 8)
        out, _, _, _ = blur_rows(d0, base)
        for t in range(9):
            img[t, pl.ds(base, 8), :] = out[t]
        return 0

    lax.fori_loop(0, 34, blur0, 0)
    clear_outside(img)

    def adjoint_parts(base):
        up, mid, down = rows_of(img, base - 1), rows_of(img, base), rows_of(img, base + 1)
        return [[kk[0][b] * down[t] + kk[1][b] * mid[t] + kk[2][b] * up[t] for t in range(9)]
                for b in range(3)]

    zero = jnp.zeros((8, 128), F32)

    def apply0(i, carry):
        gam, dad = carry
        base = pl.multiple_of(i * 8 + 16, 8)
        v = adjoint_parts(base)
        up, mid, down = rows_of(d0, base - 1), rows_of(d0, base), rows_of(d0, base + 1)
        east = sh_east(mid)
        flux = [ce[t, pl.ds(base, 8), :] * (mid[t] - east[t]) for t in range(9)]
        e0 = sh_east(v[0])
        w2_ = sh_west([v[2][t] - flux[t] for t in range(9)])
        for t in range(8):
            lap = (cs[t, pl.ds(base, 8), :] * (mid[t] - down[t])
                   - cs[t, pl.ds(base - 1, 8), :] * (up[t] - mid[t]))
            out = ((v[1][t] + e0[t]) + (w2_[t] + flux[t])) + lap
            q0[t, pl.ds(base, 8), :] = out
            gam = gam + r0[t, pl.ds(base, 8), :] * mid[t]
            dad = dad + mid[t] * out
        return gam, dad

    gam, dad = lax.fori_loop(0, 32, apply0, (zero, zero))

    src = jnp.concatenate([row_sums(q0, t) for t in range(8)], axis=1)
    hi, lo = split2(src)
    cells = jnp.dot(hi, cmat[:, 0:128], preferred_element_type=F32) + jnp.dot(
        lo, cmat[:, 0:128], preferred_element_type=F32)
    b2 = cells * ctab[5, 0, 8:40, :]
    ctab[0, 0, 8:40, :] = b2

    def q_tile(start, n):
        lanes = lax.broadcasted_iota(jnp.int32, (n, 128), 1)
        rows = pl.ds(start, n)
        return jnp.where(lanes < 64, q0[0, rows, :], q0[7, rows, :])

    tt2[0] = q_tile(16, 128).T
    tt2[1] = q_tile(144, 128).T
    tbuf[0:8, :] = b2[24:32]
    tbuf[8:40, :] = b2
    tbuf[40:48, :] = b2[0:8]
    tbuf[64:72, :] = q_tile(264, 8)
    tbuf[72:80, :] = q_tile(16, 8)
    tt2[2] = tbuf[...].T
    for t in range(8):
        sn2[t] = q0[t, 16:24, :]
        ss2[t] = q0[t, 264:272, :]
    sn2[8] = b2[0:8]
    ss2[8] = b2[24:32]
    copies2 = [(0, sn2, rs2), (1, ss2, rn2)] + side_copies(tt2, rx2, third)
    start_all(2, copies2)
    wait_recv_all(2, copies2)

    unpack_fine(rx2)
    for g in range(2):
        q0[8, 16 + 128 * g:144 + 128 * g, :] = hbuf[g].T
    tile = hbuf[2].T
    q0[8, 8:16, :] = tile[64:72]
    q0[8, 272:280, :] = tile[72:80]
    ctab[0, 1, :, :] = tile[0:48]
    for t in range(8):
        q0[t, 8:16, :] = rn2[t]
        q0[t, 272:280, :] = rs2[t]
    ctab[0, 0, 0:8, :] = rn2[8]
    ctab[0, 0, 40:48, :] = rs2[8]
    jacobi()
    precond(q0, w)

    def blur1_rim(base):
        out, _, _, _ = blur_rows(w, base)
        for t in range(9):
            img[t, pl.ds(base, 8), :] = out[t]

    def blur1(i, carry):
        qw, waw = carry
        base = pl.multiple_of(i * 8 + 16, 8)
        out, up, mid, down = blur_rows(w, base)
        east = sh_east(mid)
        flux = [ce[t, pl.ds(base, 8), :] * (mid[t] - east[t]) for t in range(9)]
        fw = sh_west(flux)
        img[8, pl.ds(base, 8), :] = out[8]
        for t in range(8):
            lap = (cs[t, pl.ds(base, 8), :] * (mid[t] - down[t])
                   - cs[t, pl.ds(base - 1, 8), :] * (up[t] - mid[t]))
            lap = lap + (flux[t] - fw[t])
            img[t, pl.ds(base, 8), :] = out[t]
            lw[t, pl.ds(base, 8), :] = lap
            qw = qw + q0[t, pl.ds(base, 8), :] * mid[t]
            waw = waw + (out[t] * out[t] + mid[t] * lap)
        return qw, waw

    blur1_rim(8)
    blur1_rim(272)
    qw, waw = lax.fori_loop(0, 32, blur1, (zero, zero))

    for n, part in enumerate((gam, dad, qw, waw)):
        red0[n:n + 1, :] = jnp.sum(part, axis=0, keepdims=True)
    red0[4:8, :] = jnp.zeros((4, 128), F32)
    redx[k8] = red0[...]
    for i in range(zk):
        @pl.when(k8 != i)
        def _():
            pltpu.make_async_remote_copy(
                red0, redx.at[k8], rsend.at[0], rrecv.at[0],
                device_id=zk_group[i], device_id_type=MESH).start()
    clear_outside(img)

    def apply1(i, _):
        base = pl.multiple_of(i * 8 + 16, 8)
        v = adjoint_parts(base)
        e0, w2_ = sh_east(v[0]), sh_west(v[2])
        for t in range(8):
            here = pl.ds(base, 8)
            lw[t, here, :] = ((v[1][t] + e0[t]) + w2_[t]) + lw[t, here, :]
        return 0

    def all_bytes(buf, n, sem):
        return pltpu.make_async_copy(buf.at[pl.ds(0, n)], buf.at[pl.ds(0, n)], sem)

    all_bytes(redx, zk - 1, rrecv.at[0]).wait()
    total = redx[0]
    for i in range(1, zk):
        total = total + redx[i]
    red1[...] = total
    redy[xy_me] = total
    for i in range(n_rows * ny):
        @pl.when(xy_me != i)
        def _():
            pltpu.make_async_remote_copy(
                red1, redy.at[xy_me], rsend.at[1], rrecv.at[1],
                device_id=xy_group[i], device_id_type=MESH).start()
    lax.fori_loop(0, 32, apply1, 0)
    all_bytes(redy, n_rows * ny - 1, rrecv.at[1]).wait()
    total = redy[0]
    for i in range(1, n_rows * ny):
        total = total + redy[i]
    value = jnp.broadcast_to(jnp.sum(total, axis=1, keepdims=True), (8, 128))
    g0 = jnp.broadcast_to(value[0:1], (8, 128))
    dq = jnp.broadcast_to(value[1:2], (8, 128))
    qws = jnp.broadcast_to(value[2:3], (8, 128))
    ws = jnp.broadcast_to(value[3:4], (8, 128))
    alpha = g0 / dq
    g1 = (g0 - alpha * dq) + alpha * (alpha * qws - dq)
    beta1 = 1.0 + g1 / g0
    dad1 = beta1 * (beta1 * dq - alpha * qws) + alpha * (alpha * ws - beta1 * qws)
    step = g1 / dad1
    ca = alpha + step * beta1
    cb = alpha * step

    stores = []
    for t in range(8):
        def finish(i, _):
            src_rows = pl.ds(pl.multiple_of(i * 8 + 16, 8), 8)
            dst_rows = pl.ds(pl.multiple_of(i * 8, 8), 8)
            sol[t, dst_rows, :] = ca * d0[t, src_rows, :] - cb * w[t, src_rows, :]
            res[t, dst_rows, :] = (r0[t, src_rows, :] - ca * q0[t, src_rows, :]) + cb * lw[t, src_rows, :]
            return 0

        lax.fori_loop(0, 32, finish, 0, unroll=4)
        lanes = pl.ds(t * 128, 128)
        stores.append(pltpu.make_async_copy(sol.at[t], sol_hbm.at[:, lanes], out_sem.at[t]))
        stores.append(pltpu.make_async_copy(res.at[t], res_hbm.at[:, lanes], out_sem.at[8 + t]))
        stores[-2].start()
        stores[-1].start()

    wait_send_all(0, copies0)
    wait_send_all(1, copies1)
    wait_send_all(2, copies2)
    all_bytes(redx, zk - 1, rsend.at[0]).wait()
    all_bytes(redy, n_rows * ny - 1, rsend.at[1]).wait()
    for x in stores:
        x.wait()


def body(n_rows, n_cols, observed, class_map, class_weights, blur_kernel):
    zk = min(8, n_cols)
    ny = n_cols // zk
    big = pltpu.VMEM((9, 288, 128), F32)
    half = pltpu.VMEM((8, 256, 128), F32)

    def v(*shape):
        return pltpu.VMEM(shape, F32)

    scratch = [
        big, pltpu.VMEM((8, 256, 128), jnp.int32), big, big, big, big, big, big, big, big, big, big,
        half, half,
        v(9, 48, 128), pltpu.VMEM((1024, 256), BF16), pltpu.VMEM((128, 1152), BF16),
        v(128, 128), v(3, 128, 128), v(3, 128, 128), v(3, 128, 128), v(3, 128, 128),
        v(6, 2, 48, 128), v(2, 64, 128),
        v(8, 8, 128), v(8, 8, 128), v(8, 8, 128), v(8, 8, 128), v(8, 3, 8, 128),
        v(5, 32, 128), v(5, 8, 128), v(5, 8, 128), v(8, 3, 8, 128),
        v(9, 8, 128), v(9, 8, 128), v(9, 8, 128), v(9, 8, 128), v(8, 3, 8, 128),
        v(8, 128), v(8, 128), v(zk, 8, 128), v(n_rows * ny, 8, 128),
        pltpu.SemaphoreType.DMA((16,)), pltpu.SemaphoreType.DMA((16,)),
        pltpu.SemaphoreType.DMA((3, 8)), pltpu.SemaphoreType.DMA((3, 8)),
        pltpu.SemaphoreType.DMA((2,)), pltpu.SemaphoreType.DMA((2,)),
    ]
    anywhere = pl.BlockSpec(memory_space=pl.ANY)
    scalars = pl.BlockSpec(memory_space=pltpu.SMEM)
    shape = jax.ShapeDtypeStruct(observed.shape, F32)
    return pl.pallas_call(
        functools.partial(kernel, n_rows, n_cols, zk),
        out_shape=(shape, shape),
        in_specs=[scalars, scalars, anywhere, anywhere],
        out_specs=(anywhere, anywhere),
        scratch_shapes=scratch,
        compiler_params=pltpu.CompilerParams(
            collective_id=0, has_side_effects=True, vmem_limit_bytes=40 * 2**20),
    )(class_weights, blur_kernel.reshape(9), observed, class_map)


def solution(mesh):
    n_rows, n_cols = mesh.shape["rows"], mesh.shape["cols"]
    return jax.shard_map(
        functools.partial(body, n_rows, n_cols),
        mesh=mesh,
        in_specs=(P("rows", "cols"), P("rows", "cols"), P(), P()),
        out_specs=(P("rows", "cols"), P("rows", "cols")),
        check_vma=False,
    )
```

time: 769 us -> 60.9 us (0.08); the launches traced: 756 us -> 60.7 us
  blocking collectives: 229 us -> 0 us
  starting transfers between devices: 190 us -> 0 us
  other arithmetic: 123 us -> 0 us
  waiting for transfers between devices: 106 us -> 0 us
  local copies, waits for them, and re-layouts: 102 us -> 5.17 us
  Pallas kernels: 0 us -> 54.9 us
    psum x3 -> x0, blocking collectives: 229 us -> none  [the longest x2 158 us: measure(): return lax.psum(jnp.sum(first * second), ('cols', 'rows'))]
    ppermute x76 -> x0, starting transfers between devices: 190 us -> none  [the longest x38 125 us: padded_2(): lax.ppermute(tail, axis, [(i, (i + 1) % count) for i in range(ends)])]
    ppermute x76 -> x0, waiting for transfers between devices: 106 us -> none  [the longest x38 98.4 us: padded_2(): lax.ppermute(head, axis, [((i + 1) % count, i) for i in range(ends)])]
    reduce_sum x9 -> x0, other arithmetic: 57.5 us -> none  [the longest x2 37.3 us: body(): jnp.sum(direction * product_field)]
    pallas_call x0 -> x1, Pallas kernels: none -> 54.9 us  [body(): pl.pallas_call(functools.partial(kernel, n_rows, n_cols, zk), out_shape=(...]
    reshape x4 -> x1, local copies, waits for them, and re-layouts: 49.6 us -> 0.77 us  [body(): blur_kernel.reshape(9)]
    add x20 -> x0, other arithmetic: 45.8 us -> none  [the longest x2 22.8 us: blurred(): summed + kernel[across, along] * padded[across:across + height, along:alo...]
    slice x31 -> x0, local copies, waits for them, and re-layouts: 22.9 us -> none  [the longest x1 6.1 us: coarse_weights(): west[:, 0::COARSE].reshape(blocks_down, COARSE, blocks_across).sum(axis=1)]
  transfers between devices with their start and end apart: 76 -> 0, of which waited for: 42 -> 0; matrix products, arithmetic and copies ran while one was open for 0% -> 0% of each run, Pallas kernels for 0% -> 0%
where the time goes in v1:
time: 60.9 us; the launch traced here: 60.7 us
  Pallas kernels  54.9 us (90%)
  local copies, waits for them, and re-layouts  5.17 us (8%)
  between operations  0.65 us (1%)
    pallas_call x1, Pallas kernels, body(): pl.pallas_call(functools.partial(kernel, n_rows, n_cols, zk), out_shape=(...  54.9 us
    unnamed x8, local copies, waits for them, and re-layouts  4.4 us

profile of v1, /device:TPU:1, one launch (start us, length us, event | category | flops | bytes accessed | tf_op | source)
XLA Modules:
  0.0 60.7 jit_solution(13727745657945343000)
XLA Ops:
  0.6 0.0 copy-start.2
  0.6 0.8 %reshape.7.bk = f32[9]{0:T(128)S(1)} reshape(f32[3,3]{1,0:T(4,128)} %param.7) | data formatting | bytes 72 | tf_op jit(solution)/shard_map/reshape | solution.py:619
  1.4 0.0 copy-done.2
  1.4 0.0 copy-start
  1.4 1.2 %copy-done = f32[256,1024]{1,0:T(8,128)S(1)} copy-done((f32[256,1024]{1,0:T(8,128)S(1)}, f32[256,1024]{1,0:T(8,128)}, u32[]{:S(2)}) %copy-start) | copy-done | bytes 1048600
  2.6 0.0 copy-start.1
  2.6 1.2 %copy-done.1 = s32[256,1024]{1,0:T(8,128)S(1)} copy-done((s32[256,1024]{1,0:T(8,128)S(1)}, s32[256,1024]{1,0:T(8,128)}, u32[]{:S(2)}) %copy-start.1) | copy-done | bytes 1048600
  3.9 54.9 %shard_map.59 = (f32[256,1024]{1,0:T(8,128)S(1)}, f32[256,1024]{1,0:T(8,128)S(1)}) custom-call(f32[4]{0:T(128)S(1)} %copy-done.2, f32[9]{0:T(128)S(1)} %reshape.7.bk, f32[256,1024]{1,0:T(8,128)S(1)} %copy-done, s32[256,1024]{1,0:T(8,128)S(1)} %copy-done.1), custom_call_target="tpu_custom_call" | custom-call | tf_op jit(solution)/shard_map/pallas_call | solution.py:611
  58.8 1.0 %copy.8 = f32[256,1024]{1,0:T(8,128)} copy(f32[256,1024]{1,0:T(8,128)S(1)} %get-tuple-element.4) | data formatting | bytes 2097152
  59.7 1.0 %copy.9 = f32[256,1024]{1,0:T(8,128)} copy(f32[256,1024]{1,0:T(8,128)S(1)} %get-tuple-element.5) | data formatting | bytes 2097152
Async XLA Ops:
  0.6 0.8 %copy-start.2 = (f32[4]{0:T(128)S(1)}, f32[4]{0:T(128)}, u32[]{:S(2)}) copy-start(f32[4]{0:T(128)} %cw.1) | copy-start | bytes 52
  1.4 1.2 %copy-start = (f32[256,1024]{1,0:T(8,128)S(1)}, f32[256,1024]{1,0:T(8,128)}, u32[]{:S(2)}) copy-start(f32[256,1024]{1,0:T(8,128)} %obs_hbm.1) | copy-start | bytes 3145732
  2.6 1.2 %copy-start.1 = (s32[256,1024]{1,0:T(8,128)S(1)}, s32[256,1024]{1,0:T(8,128)}, u32[]{:S(2)}) copy-start(s32[256,1024]{1,0:T(8,128)} %cls_hbm.1) | copy-start | bytes 3145732

commit v2 on v1

--- a/solution.py
+++ b/solution.py
@@ -13,22 +13,25 @@
 NB = ((-1, 0), (1, 0), (0, -1), (0, 1), (-1, -1), (-1, 1), (1, -1), (1, 1))
 F32 = jnp.float32
 BF16 = jnp.bfloat16
-
-
-def split2(x):
+KERNEL_VMEM = 55 * 2**20
+FINISH_VMEM = 16 * 2**20
+
+
+def exact_dot(x, ones):
     hi = x.astype(BF16)
     lo = (x - hi.astype(F32)).astype(BF16)
-    return hi, lo
+    both = jnp.dot(jnp.concatenate([hi, lo], axis=0), ones, preferred_element_type=F32)
+    return both[: x.shape[0]] + both[x.shape[0] :]
 
 
 def kernel(
     n_rows, n_cols, zk,
-    cw, bk, obs_hbm, cls_hbm, sol_hbm, res_hbm,
-    obs, cls, cond, r0, rfd, ce, cs, d0, img, q0, w, lw, sol, res,
+    cw, bk, obs_hbm, cls_hbm, r0, d0, q0, w, lw, coef,
+    obs, cls, cond, rfd, ce, cs, img,
     zup, cmat, umat, tbuf, tt0, tt1, tt2, hbuf, ctab, zs,
     sn0, ss0, rn0, rs0, rx0, sn1, rn1, rs1, rx1, sn2, ss2, rn2, rs2, rx2,
     red0, red1, redx, redy,
-    in_sem, out_sem, send_sem, recv_sem, rsend, rrecv,
+    in_sem, send_sem, recv_sem, rsend, rrecv,
 ):
     r = lax.axis_index("rows")
     c = lax.axis_index("cols")
@@ -95,7 +98,7 @@
     umat[:, 1024:1152] = jnp.where(
         ((vj < 64) & (vi == 0)) | ((vj >= 64) & (vi == 127)), 1.0, 0.0).astype(BF16)
 
-    kk = [[bk[a * 3 + b] for b in range(3)] for a in range(3)]
+    kk = [[bk[a, b] for b in range(3)] for a in range(3)]
     ksum = kk[0][0]
     ksq = kk[0][0] * kk[0][0]
     for a in range(3):
@@ -191,10 +194,30 @@
 
     third = pl.ds(2, 1)
     copies0 = [(0, sn0, rs0), (1, ss0, rn0)] + side_copies(tt0, rx0, third)
-
     pl.semaphore_wait(bar, peers)
-
     start_all(0, copies0)
+
+    def blur_adjoint(up, mid, down, b):
+        return kk[0][b] * down + kk[1][b] * mid + kk[2][b] * up
+
+    def own_body(i, _):
+        base = pl.multiple_of(i * 8 + 24, 8)
+        here = pl.ds(base, 8)
+        up, mid, down = rows_of(obs, base - 1, 8), rows_of(obs, base, 8), rows_of(obs, base + 1, 8)
+        v = [[blur_adjoint(up[t], mid[t], down[t], b) for t in range(8)] for b in range(3)]
+        e0 = [pltpu.roll(x, 127, 1) for x in v[0]]
+        w2_ = [pltpu.roll(x, 1, 1) for x in v[2]]
+        cm, csouth = rows_of(cond, base, 8), rows_of(cond, base + 1, 8)
+        ceast = [pltpu.roll(x, 127, 1) for x in cm]
+        for t in range(8):
+            e = jnp.where(last_lane, e0[t + 1] if t < 7 else 0.0, e0[t])
+            w_ = jnp.where(first_lane, w2_[t - 1] if t else 0.0, w2_[t])
+            r0[t, here, :] = v[1][t] + e + w_
+            ce[t, here, :] = 0.5 * (cm[t] + jnp.where(last_lane, ceast[t + 1] if t < 7 else 0.0, ceast[t]))
+            cs[t, here, :] = 0.5 * (cm[t] + csouth[t])
+        return 0
+
+    lax.fori_loop(0, 30, own_body, 0, unroll=3)
     wait_recv_all(0, copies0)
 
     def side(rx, group, dc, in_north, in_center):
@@ -235,31 +258,41 @@
         obs[t, 272:280, :] = rs0[t]
         cond[t, 272:280, :] = pltpu.roll(rs0[t], 4, 0)
 
-    def fine_body(i, _):
-        base = pl.multiple_of(i * 8 + 8, 8)
+    def side_body(i, _):
+        base = pl.multiple_of(i * 8 + 24, 8)
+        here = pl.ds(base, 8)
+        def v(t, b):
+            return blur_adjoint(obs[t, pl.ds(base - 1, 8), :], obs[t, here, :],
+                                obs[t, pl.ds(base + 1, 8), :], b)
+        e8, w8 = pltpu.roll(v(8, 0), 127, 1), pltpu.roll(v(8, 2), 1, 1)
+        e0, w7 = pltpu.roll(v(0, 0), 127, 1), pltpu.roll(v(7, 2), 1, 1)
+        r0[8, here, :] = v(8, 1) + jnp.where(last_lane, e0, e8) + jnp.where(first_lane, w7, w8)
+        r0[7, here, :] = r0[7, here, :] + jnp.where(last_lane, e8, 0.0)
+        r0[0, here, :] = r0[0, here, :] + jnp.where(first_lane, w8, 0.0)
+        c8 = cond[8, here, :]
+        ce8, ce0 = pltpu.roll(c8, 127, 1), pltpu.roll(cond[0, here, :], 127, 1)
+        ce[8, here, :] = 0.5 * (c8 + jnp.where(last_lane, ce0, ce8))
+        ce[7, here, :] = ce[7, here, :] + 0.5 * jnp.where(last_lane, ce8, 0.0)
+        cs[8, here, :] = 0.5 * (c8 + cond[8, pl.ds(base + 1, 8), :])
+        return 0
+
+    lax.fori_loop(0, 30, side_body, 0, unroll=6)
+
+    def outer_body(i, _):
+        base = pl.multiple_of(jnp.where(i < 2, i * 8 + 8, i * 8 + 248), 8)
+        here = pl.ds(base, 8)
         up, mid, down = rows_of(obs, base - 1), rows_of(obs, base), rows_of(obs, base + 1)
-        v = [[kk[0][b] * down[t] + kk[1][b] * mid[t] + kk[2][b] * up[t] for t in range(9)]
-             for b in range(3)]
+        v = [[blur_adjoint(up[t], mid[t], down[t], b) for t in range(9)] for b in range(3)]
         e0, w2_ = sh_east(v[0]), sh_west(v[2])
+        cm, csouth = rows_of(cond, base), rows_of(cond, base + 1)
+        ceast = sh_east(cm)
         for t in range(9):
-            r0[t, pl.ds(base, 8), :] = v[1][t] + e0[t] + w2_[t]
+            r0[t, here, :] = v[1][t] + e0[t] + w2_[t]
+            ce[t, here, :] = 0.5 * (cm[t] + ceast[t])
+            cs[t, here, :] = 0.5 * (cm[t] + csouth[t])
         return 0
 
-    lax.fori_loop(0, 34, fine_body, 0)
-
-    def edge_body(i, _):
-        base = pl.multiple_of(i * 8 + 8, 8)
-        north, mid, south = rows_of(cond, base - 1), rows_of(cond, base), rows_of(cond, base + 1)
-        east, west = sh_east(mid), sh_west(mid)
-        for t in range(9):
-            here = pl.ds(base, 8)
-            total = (east[t] + west[t]) + (north[t] + south[t])
-            rfd[t, here, :] = 1.0 / (ksq + 2.0 * mid[t] + 0.5 * total)
-            ce[t, here, :] = 0.5 * (mid[t] + east[t])
-            cs[t, here, :] = 0.5 * (mid[t] + south[t])
-        return 0
-
-    lax.fori_loop(0, 34, edge_body, 0)
+    lax.fori_loop(0, 4, outer_body, 0, unroll=2)
 
     def clear_outside(ref):
         @pl.when(r == 0)
@@ -281,8 +314,6 @@
         @pl.when(c == n_cols - 1)
         def _():
             ref[8, 8:280, :] = jnp.where(lanes >= 64, ref[8, 8:280, :], 0.0)
-
-    clear_outside(rfd)
 
     def row_sums(ref, t):
         total = ref[t, pl.ds(16, 32, stride=8), :]
@@ -295,9 +326,7 @@
     srow = jnp.concatenate([cs[t, pl.ds(23, 32, stride=8), :] for t in range(8)], axis=1)
     nrow = jnp.concatenate([cs[t, 8:16, :] for t in range(8)], axis=1)
     stack = jnp.concatenate([src, esum, srow, nrow], axis=0)
-    hi, lo = split2(stack)
-    sums = jnp.dot(hi, cmat[...], preferred_element_type=F32) + jnp.dot(
-        lo, cmat[...], preferred_element_type=F32)
+    sums = exact_dot(stack, cmat[...])
     source = sums[0:32, 0:128]
     c_east = sums[32:64, 128:256]
     c_south = sums[64:96, 0:128]
@@ -328,6 +357,19 @@
     copies1 = [(0, sn1.at[:, pl.ds(0, 8), :], rs1), (1, sn1.at[:, pl.ds(24, 8), :], rn1)]
     copies1 += side_copies(tt1, rx1, whole)
     start_all(1, copies1)
+
+    def diag_body(i, _):
+        base = pl.multiple_of(i * 8 + 8, 8)
+        here = pl.ds(base, 8)
+        east = rows_of(ce, base)
+        west = sh_west(east)
+        for t in range(9):
+            total = (east[t] + west[t]) + (cs[t, here, :] + cs[t, pl.ds(base - 1, 8), :])
+            rfd[t, here, :] = 1.0 / (ksq + total)
+        return 0
+
+    lax.fori_loop(0, 34, diag_body, 0, unroll=4)
+    clear_outside(rfd)
     wait_recv_all(1, copies1)
 
     for f in range(5):
@@ -365,14 +407,10 @@
         for t in range(2):
             zs[t, 8:56, :] = ctab[0, t]
         lax.fori_loop(0, SWEEPS - 1, sweep, 0)
-        hi0, lo0 = split2(zs[0, 8:56, :])
-        hi1, lo1 = split2(zs[1, 8:56, :])
-        up = jnp.dot(hi0, umat[:, 0:1024], preferred_element_type=F32) + jnp.dot(
-            lo0, umat[:, 0:1024], preferred_element_type=F32)
+        up = exact_dot(zs[0, 8:56, :], umat[:, 0:1024])
         for t in range(8):
             zup[t] = up[:, 128 * t:128 * t + 128]
-        zup[8] = jnp.dot(hi1, umat[:, 1024:1152], preferred_element_type=F32) + jnp.dot(
-            lo1, umat[:, 1024:1152], preferred_element_type=F32)
+        zup[8] = exact_dot(zs[1, 8:56, :], umat[:, 1024:1152])
 
     jacobi()
 
@@ -384,7 +422,7 @@
                 out[t, here, :] = field[t, here, :] * rfd[t, here, :] + zup[t, pl.ds(i + 7, 1), :]
             return 0
 
-        lax.fori_loop(0, 34, body, 0)
+        lax.fori_loop(0, 34, body, 0, unroll=4)
 
     precond(r0, d0)
 
@@ -402,7 +440,7 @@
             img[t, pl.ds(base, 8), :] = out[t]
         return 0
 
-    lax.fori_loop(0, 34, blur0, 0)
+    lax.fori_loop(0, 34, blur0, 0, unroll=4)
     clear_outside(img)
 
     def adjoint_parts(base):
@@ -430,12 +468,10 @@
             dad = dad + mid[t] * out
         return gam, dad
 
-    gam, dad = lax.fori_loop(0, 32, apply0, (zero, zero))
+    gam, dad = lax.fori_loop(0, 32, apply0, (zero, zero), unroll=4)
 
     src = jnp.concatenate([row_sums(q0, t) for t in range(8)], axis=1)
-    hi, lo = split2(src)
-    cells = jnp.dot(hi, cmat[:, 0:128], preferred_element_type=F32) + jnp.dot(
-        lo, cmat[:, 0:128], preferred_element_type=F32)
+    cells = exact_dot(src, cmat[:, 0:128])
     b2 = cells * ctab[5, 0, 8:40, :]
     ctab[0, 0, 8:40, :] = b2
 
@@ -501,7 +537,7 @@
 
     blur1_rim(8)
     blur1_rim(272)
-    qw, waw = lax.fori_loop(0, 32, blur1, (zero, zero))
+    qw, waw = lax.fori_loop(0, 32, blur1, (zero, zero), unroll=4)
 
     for n, part in enumerate((gam, dad, qw, waw)):
         red0[n:n + 1, :] = jnp.sum(part, axis=0, keepdims=True)
@@ -539,7 +575,7 @@
             pltpu.make_async_remote_copy(
                 red1, redy.at[xy_me], rsend.at[1], rrecv.at[1],
                 device_id=xy_group[i], device_id_type=MESH).start()
-    lax.fori_loop(0, 32, apply1, 0)
+    lax.fori_loop(0, 32, apply1, 0, unroll=4)
     all_bytes(redy, n_rows * ny - 1, rrecv.at[1]).wait()
     total = redy[0]
     for i in range(1, n_rows * ny):
@@ -557,6 +593,17 @@
     ca = alpha + step * beta1
     cb = alpha * step
 
+    coef[0] = ca
+    coef[1] = cb
+    wait_send_all(0, copies0)
+    wait_send_all(1, copies1)
+    wait_send_all(2, copies2)
+    all_bytes(redx, zk - 1, rsend.at[0]).wait()
+    all_bytes(redy, n_rows * ny - 1, rsend.at[1]).wait()
+
+
+def finish_kernel(r0, d0, q0, w, lw, coef, sol_hbm, res_hbm, sol, res, out_sem):
+    ca, cb = coef[0], coef[1]
     stores = []
     for t in range(8):
         def finish(i, _):
@@ -566,18 +613,12 @@
             res[t, dst_rows, :] = (r0[t, src_rows, :] - ca * q0[t, src_rows, :]) + cb * lw[t, src_rows, :]
             return 0
 
-        lax.fori_loop(0, 32, finish, 0, unroll=4)
+        lax.fori_loop(0, 32, finish, 0, unroll=8)
         lanes = pl.ds(t * 128, 128)
         stores.append(pltpu.make_async_copy(sol.at[t], sol_hbm.at[:, lanes], out_sem.at[t]))
         stores.append(pltpu.make_async_copy(res.at[t], res_hbm.at[:, lanes], out_sem.at[8 + t]))
         stores[-2].start()
         stores[-1].start()
-
-    wait_send_all(0, copies0)
-    wait_send_all(1, copies1)
-    wait_send_all(2, copies2)
-    all_bytes(redx, zk - 1, rsend.at[0]).wait()
-    all_bytes(redy, n_rows * ny - 1, rsend.at[1]).wait()
     for x in stores:
         x.wait()
 
@@ -592,8 +633,7 @@
         return pltpu.VMEM(shape, F32)
 
     scratch = [
-        big, pltpu.VMEM((8, 256, 128), jnp.int32), big, big, big, big, big, big, big, big, big, big,
-        half, half,
+        big, pltpu.VMEM((8, 256, 128), jnp.int32), big, big, big, big, big,
         v(9, 48, 128), pltpu.VMEM((1024, 256), BF16), pltpu.VMEM((128, 1152), BF16),
         v(128, 128), v(3, 128, 128), v(3, 128, 128), v(3, 128, 128), v(3, 128, 128),
         v(6, 2, 48, 128), v(2, 64, 128),
@@ -601,22 +641,32 @@
         v(5, 32, 128), v(5, 8, 128), v(5, 8, 128), v(8, 3, 8, 128),
         v(9, 8, 128), v(9, 8, 128), v(9, 8, 128), v(9, 8, 128), v(8, 3, 8, 128),
         v(8, 128), v(8, 128), v(zk, 8, 128), v(n_rows * ny, 8, 128),
-        pltpu.SemaphoreType.DMA((16,)), pltpu.SemaphoreType.DMA((16,)),
+        pltpu.SemaphoreType.DMA((16,)),
         pltpu.SemaphoreType.DMA((3, 8)), pltpu.SemaphoreType.DMA((3, 8)),
         pltpu.SemaphoreType.DMA((2,)), pltpu.SemaphoreType.DMA((2,)),
     ]
-    anywhere = pl.BlockSpec(memory_space=pl.ANY)
+    hbm = pl.BlockSpec(memory_space=pltpu.HBM)
+    vmem = pl.BlockSpec(memory_space=pltpu.VMEM)
     scalars = pl.BlockSpec(memory_space=pltpu.SMEM)
+    field = pltpu.VMEM((9, 288, 128), F32)
+    fields = pl.pallas_call(
+        functools.partial(kernel, n_rows, n_cols, zk),
+        out_shape=(field,) * 5 + (pltpu.VMEM((2, 8, 128), F32),),
+        in_specs=[scalars, scalars, hbm, hbm],
+        out_specs=(vmem,) * 6,
+        scratch_shapes=scratch,
+        compiler_params=pltpu.CompilerParams(
+            collective_id=0, has_side_effects=True, vmem_limit_bytes=KERNEL_VMEM),
+    )(class_weights, blur_kernel, observed, class_map)
     shape = jax.ShapeDtypeStruct(observed.shape, F32)
     return pl.pallas_call(
-        functools.partial(kernel, n_rows, n_cols, zk),
+        finish_kernel,
         out_shape=(shape, shape),
-        in_specs=[scalars, scalars, anywhere, anywhere],
-        out_specs=(anywhere, anywhere),
-        scratch_shapes=scratch,
-        compiler_params=pltpu.CompilerParams(
-            collective_id=0, has_side_effects=True, vmem_limit_bytes=40 * 2**20),
-    )(class_weights, blur_kernel.reshape(9), observed, class_map)
+        in_specs=[vmem] * 6,
+        out_specs=(hbm, hbm),
+        scratch_shapes=[half, half, pltpu.SemaphoreType.DMA((16,))],
+        compiler_params=pltpu.CompilerParams(vmem_limit_bytes=FINISH_VMEM),
+    )(*fields)
 
 
 def solution(mesh):

time: 60.9 us -> 42.1 us (0.69)
  Pallas kernels: 54.9 us -> 41.3 us
  local copies, waits for them, and re-layouts: 5.17 us -> 0 us
    pallas_call x1, Pallas kernels: 54.9 us -> 39.8 us  [body(): pl.pallas_call(functools.partial(kernel, n_rows, n_cols, zk), out_shape=(...]
    unnamed x8 -> x0, local copies, waits for them, and re-layouts: 4.4 us -> none
    pallas_call x0 -> x1, Pallas kernels: none -> 1.49 us  [body(): pl.pallas_call(finish_kernel, out_shape=(shape, shape), in_specs=[vmem] *...]
    reshape x1 -> x0, local copies, waits for them, and re-layouts: 0.77 us -> none  [body(): blur_kernel.reshape(9)]
where the time goes in v2:
time: 42.1 us; the launch traced here: 42 us
  Pallas kernels  41.3 us (98%)
  between operations  0.64 us (2%)
    pallas_call x1, Pallas kernels, body(): pl.pallas_call(functools.partial(kernel, n_rows, n_cols, zk), out_shape=(...  39.8 us
    pallas_call x1, Pallas kernels, body(): pl.pallas_call(finish_kernel, out_shape=(shape, shape), in_specs=[vmem] *...  1.49 us

profile of v2, /device:TPU:1, one launch (start us, length us, event | category | flops | bytes accessed | tf_op | source)
XLA Modules:
  0.0 42.0 jit_solution(14852857089319841751)
XLA Ops:
  0.6 39.8 %shard_map.59 = (f32[9,288,128]{2,1,0:T(8,128)S(1)}, f32[9,288,128]{2,1,0:T(8,128)S(1)}, f32[9,288,128]{2,1,0:T(8,128)S(1)}, f32[9,288,128]{2,1,0:T(8,128)S(1)},...) custom-call(f32[4]{0:T(128)} %cw.1, f32[3,3]{1,0:T(4,128)} %bk.1, f32[256,1024]{1,0:T(8,128)} %obs_hbm.1, ...), custom_call_target="tpu_custom_call" | custom-call | tf_op jit(solution)/shard_map/pallas_call | solution.py:652
  40.5 1.5 %shard_map.60 = (f32[256,1024]{1,0:T(8,128)}, f32[256,1024]{1,0:T(8,128)}) custom-call(f32[9,288,128]{2,1,0:T(8,128)S(1)} %get-tuple-element.8.r0, f32[9,288,128]{2,1,0:T(8,128)S(1)} %get-tuple-element.9.d0, f32[9,288,128]{2,1,0:T(8,128)S(1)} %get-tuple-element.10.q0, f32[9,288,128]{2,1,0:T(8,128)S(1)} %get-tuple-element.11.w, ...), custom_call_target="tpu_custom_call" | custom-call | tf_op jit(solution)/shard_map/pallas_call | solution.py:662

commit v3 on v2

--- a/solution.py
+++ b/solution.py
@@ -29,7 +29,7 @@
     cw, bk, obs_hbm, cls_hbm, r0, d0, q0, w, lw, coef,
     obs, cls, cond, rfd, ce, cs, img,
     zup, cmat, umat, tbuf, tt0, tt1, tt2, hbuf, ctab, zs,
-    sn0, ss0, rn0, rs0, rx0, sn1, rn1, rs1, rx1, sn2, ss2, rn2, rs2, rx2,
+    rx0, sn1, rn1, rs1, rx1, sn2, rn2, rs2, rx2, zeast, zwest,
     red0, red1, redx, redy,
     in_sem, send_sem, recv_sem, rsend, rrecv,
 ):
@@ -53,8 +53,12 @@
     for x in loads:
         x.start()
 
-    for buf in (rn0, rs0, rx0, rn1, rs1, rx1, rn2, rs2, rx2, hbuf, zs):
+    for buf in (rx0, rn1, rs1, rx1, rn2, rs2, rx2, hbuf, zs):
         buf[...] = jnp.zeros(buf.shape, F32)
+    for buf in (obs, cond):
+        for t in range(8):
+            buf[t, 8:16, :] = jnp.zeros((8, 128), F32)
+            buf[t, 272:280, :] = jnp.zeros((8, 128), F32)
 
     bar = pltpu.get_barrier_semaphore()
     peers = zk + n_rows * ny - 2
@@ -69,22 +73,126 @@
         @pl.when(fresh)
         def _():
             pl.semaphore_signal(bar, inc=1, device_id=dev(dr, dc), device_id_type=MESH)
-    zk_group = [(y * zk + i, r) for i in range(zk)]
+    nz = zk // 2
+    z_me, core = k8 // 2, lax.rem(k8, 2)
     xy_me = r * ny + y
-    xy_group = [(j * zk + k8, i) for i in range(n_rows) for j in range(ny)]
-    for i in range(zk):
-        @pl.when(k8 != i)
-        def _():
-            pl.semaphore_signal(bar, inc=1, device_id=zk_group[i], device_id_type=MESH)
-    for i in range(n_rows * ny):
-        @pl.when(xy_me != i)
-        def _():
-            pl.semaphore_signal(bar, inc=1, device_id=xy_group[i], device_id_type=MESH)
+
+    def ring(o, n):
+        return min(o, n - o)
+
+    zk_far = sorted(((a, b) for a in range(nz) for b in range(2) if a or b),
+                    key=lambda o: -(2 * ring(o[0], nz) + o[1]))
+    xy_far = sorted(((a, b) for a in range(n_rows) for b in range(ny) if a or b),
+                    key=lambda o: -(ring(o[0], n_rows) + ring(o[1], ny)))
+    zk_group = [(y * zk + lax.rem(z_me + a, nz) * 2 + lax.rem(core + b, 2), r) for a, b in zk_far]
+    xy_group = [(lax.rem(y + b, ny) * zk + k8, lax.rem(r + a, n_rows)) for a, b in xy_far]
+    for peer in zk_group + xy_group:
+        pl.semaphore_signal(bar, inc=1, device_id=peer, device_id_type=MESH)
 
     lane = lax.broadcasted_iota(jnp.int32, (8, 128), 1)
     sub = lax.broadcasted_iota(jnp.int32, (8, 128), 0)
     first_lane = lane == 0
     last_lane = lane == 127
+
+    kk = [[bk[a, b] for b in range(3)] for a in range(3)]
+    ksum = kk[0][0]
+    ksq = kk[0][0] * kk[0][0]
+    for a in range(3):
+        for b in range(3):
+            if a + b:
+                ksum = ksum + kk[a][b]
+                ksq = ksq + kk[a][b] * kk[a][b]
+
+    def sh_east(v):
+        rolled = [pltpu.roll(x, 127, 1) for x in v]
+        n = len(v)
+        return [jnp.where(last_lane, rolled[(t + 1) % n], rolled[t]) for t in range(n)]
+
+    def sh_west(v):
+        rolled = [pltpu.roll(x, 1, 1) for x in v]
+        n = len(v)
+        return [jnp.where(first_lane, rolled[(t - 1) % n], rolled[t]) for t in range(n)]
+
+    def rows_of(ref, base, n=9):
+        return [ref[t, pl.ds(base, 8), :] for t in range(n)]
+
+    for x in loads:
+        x.wait()
+
+    w0, w1, w2, w3 = cw[0], cw[1], cw[2], cw[3]
+
+    def cond_body(i, _):
+        src = pl.multiple_of(i * 8, 8)
+        dst = pl.multiple_of(i * 8 + 16, 8)
+        for t in range(8):
+            m = cls[t, pl.ds(src, 8), :]
+            cond[t, pl.ds(dst, 8), :] = jnp.where(
+                m == 0, w0, jnp.where(m == 1, w1, jnp.where(m == 2, w2, w3)))
+        return 0
+
+    lax.fori_loop(0, 32, cond_body, 0)
+
+    def rim_tile(start, n):
+        lanes = lax.broadcasted_iota(jnp.int32, (n, 128), 1)
+        rows = pl.ds(start, n)
+        left = jnp.where(lanes < 8, obs[0, rows, :], pltpu.roll(cond[0, rows, :], 8, 1))
+        right = jnp.where(lanes >= 120, obs[7, rows, :], pltpu.roll(cond[7, rows, :], 120, 1))
+        return jnp.where(lanes < 64, left, right)
+
+    tt0[0] = rim_tile(16, 128).T
+    tt0[1] = rim_tile(144, 128).T
+    tbuf[...] = jnp.zeros(tbuf.shape, F32)
+    tbuf[64:72, :] = rim_tile(264, 8)
+    tbuf[72:80, :] = rim_tile(16, 8)
+    tt0[2] = tbuf[...].T
+
+    def side_copies(tt, rx, groups_diag, width):
+        low, high = pl.ds(0, width), pl.ds(128 - width, width)
+        out = []
+        for n, (dr, dc) in enumerate(NB):
+            if dc == 0:
+                continue
+            groups = pl.ds(0, tt.shape[0]) if dr == 0 else groups_diag
+            rows = low if dc < 0 else high
+            out.append((n, n, tt.at[groups, rows, :], rx.at[n, groups]))
+        return out
+
+    def start_all(phase, copies):
+        for q, n, src, dst in copies:
+            dr, dc = NB[n]
+            @pl.when(ok(dr, dc))
+            def _():
+                pltpu.make_async_remote_copy(
+                    src, dst, send_sem.at[phase, q], recv_sem.at[phase, q],
+                    device_id=dev(dr, dc), device_id_type=MESH).start()
+
+    def wait_recv_all(phase, copies):
+        for q, n, src, dst in copies:
+            dr, dc = NB[n]
+            @pl.when(ok(-dr, -dc))
+            def _():
+                pltpu.make_async_remote_copy(
+                    src, dst, send_sem.at[phase, q], recv_sem.at[phase, q],
+                    device_id=dev(-dr, -dc), device_id_type=MESH).wait_recv()
+
+    def wait_send_all(phase, copies):
+        for q, n, src, dst in copies:
+            dr, dc = NB[n]
+            @pl.when(ok(dr, dc))
+            def _():
+                pltpu.make_async_remote_copy(
+                    src, dst, send_sem.at[phase, q], recv_sem.at[phase, q],
+                    device_id=dev(dr, dc), device_id_type=MESH).wait_send()
+
+    third = pl.ds(2, 1)
+    own, top, low = pl.ds(0, 8), pl.ds(16, 8), pl.ds(264, 8)
+    above, below = pl.ds(8, 8), pl.ds(272, 8)
+    copies0 = side_copies(tt0, rx0, third, 16)
+    for q, field in ((0, obs), (8, cond)):
+        copies0.append((q, 0, field.at[own, top, :], field.at[own, below, :]))
+        copies0.append((q + 1, 1, field.at[own, low, :], field.at[own, above, :]))
+    pl.semaphore_wait(bar, peers)
+    start_all(0, copies0)
 
     ii = lax.broadcasted_iota(jnp.int32, (1024, 128), 0)
     jj = lax.broadcasted_iota(jnp.int32, (1024, 128), 1)
@@ -98,105 +206,6 @@
     umat[:, 1024:1152] = jnp.where(
         ((vj < 64) & (vi == 0)) | ((vj >= 64) & (vi == 127)), 1.0, 0.0).astype(BF16)
 
-    kk = [[bk[a, b] for b in range(3)] for a in range(3)]
-    ksum = kk[0][0]
-    ksq = kk[0][0] * kk[0][0]
-    for a in range(3):
-        for b in range(3):
-            if a + b:
-                ksum = ksum + kk[a][b]
-                ksq = ksq + kk[a][b] * kk[a][b]
-
-    def sh_east(v):
-        rolled = [pltpu.roll(x, 127, 1) for x in v]
-        n = len(v)
-        return [jnp.where(last_lane, rolled[(t + 1) % n], rolled[t]) for t in range(n)]
-
-    def sh_west(v):
-        rolled = [pltpu.roll(x, 1, 1) for x in v]
-        n = len(v)
-        return [jnp.where(first_lane, rolled[(t - 1) % n], rolled[t]) for t in range(n)]
-
-    def rows_of(ref, base, n=9):
-        return [ref[t, pl.ds(base, 8), :] for t in range(n)]
-
-    for x in loads:
-        x.wait()
-
-    w0, w1, w2, w3 = cw[0], cw[1], cw[2], cw[3]
-
-    def cond_body(i, _):
-        src = pl.multiple_of(i * 8, 8)
-        dst = pl.multiple_of(i * 8 + 16, 8)
-        for t in range(8):
-            m = cls[t, pl.ds(src, 8), :]
-            cond[t, pl.ds(dst, 8), :] = jnp.where(
-                m == 0, w0, jnp.where(m == 1, w1, jnp.where(m == 2, w2, w3)))
-        return 0
-
-    lax.fori_loop(0, 32, cond_body, 0)
-
-    for t in range(8):
-        sn0[t] = jnp.where(sub < 4, obs[t, 16:24, :], pltpu.roll(cond[t, 16:24, :], 4, 0))
-        ss0[t] = jnp.where(sub >= 4, obs[t, 264:272, :], pltpu.roll(cond[t, 264:272, :], 4, 0))
-
-    def rim_tile(start, n):
-        lanes = lax.broadcasted_iota(jnp.int32, (n, 128), 1)
-        rows = pl.ds(start, n)
-        left = jnp.where(lanes < 4, obs[0, rows, :], pltpu.roll(cond[0, rows, :], 4, 1))
-        right = jnp.where(lanes >= 124, obs[7, rows, :], pltpu.roll(cond[7, rows, :], 124, 1))
-        return jnp.where(lanes < 64, left, right)
-
-    tt0[0] = rim_tile(16, 128).T
-    tt0[1] = rim_tile(144, 128).T
-    tbuf[...] = jnp.zeros(tbuf.shape, F32)
-    tbuf[64:72, :] = rim_tile(264, 8)
-    tbuf[72:80, :] = rim_tile(16, 8)
-    tt0[2] = tbuf[...].T
-
-    def side_copies(tt, rx, groups_diag):
-        low, high = pl.ds(0, 8), pl.ds(120, 8)
-        out = []
-        for n, (dr, dc) in enumerate(NB):
-            if dc == 0:
-                continue
-            groups = pl.ds(0, 3) if dr == 0 else groups_diag
-            rows = low if dc < 0 else high
-            out.append((n, tt.at[groups, rows, :], rx.at[n, groups]))
-        return out
-
-    def start_all(phase, copies):
-        for n, src, dst in copies:
-            dr, dc = NB[n]
-            @pl.when(ok(dr, dc))
-            def _():
-                pltpu.make_async_remote_copy(
-                    src, dst, send_sem.at[phase, n], recv_sem.at[phase, n],
-                    device_id=dev(dr, dc), device_id_type=MESH).start()
-
-    def wait_recv_all(phase, copies):
-        for n, src, dst in copies:
-            dr, dc = NB[n]
-            @pl.when(ok(-dr, -dc))
-            def _():
-                pltpu.make_async_remote_copy(
-                    src, dst, send_sem.at[phase, n], recv_sem.at[phase, n],
-                    device_id=dev(-dr, -dc), device_id_type=MESH).wait_recv()
-
-    def wait_send_all(phase, copies):
-        for n, src, dst in copies:
-            dr, dc = NB[n]
-            @pl.when(ok(dr, dc))
-            def _():
-                pltpu.make_async_remote_copy(
-                    src, dst, send_sem.at[phase, n], recv_sem.at[phase, n],
-                    device_id=dev(dr, dc), device_id_type=MESH).wait_send()
-
-    third = pl.ds(2, 1)
-    copies0 = [(0, sn0, rs0), (1, ss0, rn0)] + side_copies(tt0, rx0, third)
-    pl.semaphore_wait(bar, peers)
-    start_all(0, copies0)
-
     def blur_adjoint(up, mid, down, b):
         return kk[0][b] * down + kk[1][b] * mid + kk[2][b] * up
 
@@ -226,22 +235,18 @@
         south = rx[NB.index((-1, dc)), group]
         return jnp.where(in_north, north, jnp.where(in_center, center, south))
 
-    fine_north = (lane < 8) | ((lane >= 64) & (lane < 72))
-    fine_center = (lane >= 8) & (lane < 40)
     lane64 = lax.rem(lane, 64)
 
-    def unpack_fine(rx):
-        for dc, rows in ((-1, slice(0, 8)), (1, slice(120, 128))):
-            here = NB.index((0, dc))
-            hbuf[0, rows, :] = rx[here, 0]
-            hbuf[1, rows, :] = rx[here, 1]
-            hbuf[2, rows, :] = side(rx, 2, dc, fine_north, fine_center)
-
-    unpack_fine(rx0)
+    lane16 = lax.broadcasted_iota(jnp.int32, (16, 128), 1)
+    for dc, rows in ((-1, slice(0, 16)), (1, slice(112, 128))):
+        here = NB.index((0, dc))
+        hbuf[0, rows, :] = rx0[here, 0]
+        hbuf[1, rows, :] = rx0[here, 1]
+        hbuf[2, rows, :] = side(rx0, 2, dc, lane16 < 72, lane16 < 0)
 
     def cond_of(x):
         lanes = lax.broadcasted_iota(jnp.int32, x.shape, 1)
-        return jnp.where(lanes < 64, pltpu.roll(x, 124, 1), pltpu.roll(x, 4, 1))
+        return jnp.where(lanes < 64, pltpu.roll(x, 120, 1), pltpu.roll(x, 8, 1))
 
     for g in range(2):
         tile = hbuf[g].T
@@ -252,12 +257,6 @@
     for rows, lo in ((slice(8, 16), 64), (slice(272, 280), 72)):
         obs[8, rows, :] = tile[lo:lo + 8]
         cond[8, rows, :] = cond_of(tile[lo:lo + 8])
-    for t in range(8):
-        obs[t, 8:16, :] = rn0[t]
-        cond[t, 8:16, :] = pltpu.roll(rn0[t], 4, 0)
-        obs[t, 272:280, :] = rs0[t]
-        cond[t, 272:280, :] = pltpu.roll(rs0[t], 4, 0)
-
     def side_body(i, _):
         base = pl.multiple_of(i * 8 + 24, 8)
         here = pl.ds(base, 8)
@@ -341,6 +340,7 @@
     scale = OMEGA / c_diag
     fields = (source * scale, c_east * scale, c_west * scale, c_north * scale, c_south * scale)
     ctab[5, 0, 8:40, :] = scale
+    ctab[5, 1, 8:40, :] = c_diag * (1.0 / OMEGA)
     for f in range(5):
         ctab[f, 0, 8:40, :] = fields[f]
         sn1[f] = fields[f]
@@ -354,8 +354,8 @@
         tt1[g] = tbuf[...].T
 
     whole = pl.ds(0, 3)
-    copies1 = [(0, sn1.at[:, pl.ds(0, 8), :], rs1), (1, sn1.at[:, pl.ds(24, 8), :], rn1)]
-    copies1 += side_copies(tt1, rx1, whole)
+    copies1 = [(0, 0, sn1.at[:, pl.ds(0, 8), :], rs1), (1, 1, sn1.at[:, pl.ds(24, 8), :], rn1)]
+    copies1 += side_copies(tt1, rx1, whole, 8)
     start_all(1, copies1)
 
     def diag_body(i, _):
@@ -375,6 +375,8 @@
     for f in range(5):
         ctab[f, 0, 0:8, :] = rn1[f]
         ctab[f, 0, 40:48, :] = rs1[f]
+    hbuf[:, 8:16, :] = jnp.zeros((3, 8, 128), F32)
+    hbuf[:, 112:120, :] = jnp.zeros((3, 8, 128), F32)
     for g in range(3):
         for dc, rows in ((-1, slice(0, 8)), (1, slice(120, 128))):
             hbuf[g, rows, :] = side(rx1, g, dc, lane64 < 8, lane64 < 40)
@@ -407,12 +409,15 @@
         for t in range(2):
             zs[t, 8:56, :] = ctab[0, t]
         lax.fori_loop(0, SWEEPS - 1, sweep, 0)
+
+    def spread():
         up = exact_dot(zs[0, 8:56, :], umat[:, 0:1024])
         for t in range(8):
             zup[t] = up[:, 128 * t:128 * t + 128]
         zup[8] = exact_dot(zs[1, 8:56, :], umat[:, 1024:1152])
 
     jacobi()
+    spread()
 
     def precond(field, out):
         def body(i, _):
@@ -443,29 +448,32 @@
     lax.fori_loop(0, 34, blur0, 0, unroll=4)
     clear_outside(img)
 
-    def adjoint_parts(base):
+    def apply_rows(field, base, n):
         up, mid, down = rows_of(img, base - 1), rows_of(img, base), rows_of(img, base + 1)
-        return [[kk[0][b] * down[t] + kk[1][b] * mid[t] + kk[2][b] * up[t] for t in range(9)]
-                for b in range(3)]
-
-    zero = jnp.zeros((8, 128), F32)
-
-    def apply0(i, carry):
-        gam, dad = carry
-        base = pl.multiple_of(i * 8 + 16, 8)
-        v = adjoint_parts(base)
-        up, mid, down = rows_of(d0, base - 1), rows_of(d0, base), rows_of(d0, base + 1)
+        v = [[blur_adjoint(up[t], mid[t], down[t], b) for t in range(9)] for b in range(3)]
+        up, mid, down = rows_of(field, base - 1), rows_of(field, base), rows_of(field, base + 1)
         east = sh_east(mid)
         flux = [ce[t, pl.ds(base, 8), :] * (mid[t] - east[t]) for t in range(9)]
         e0 = sh_east(v[0])
         w2_ = sh_west([v[2][t] - flux[t] for t in range(9)])
-        for t in range(8):
+        out = []
+        for t in range(n):
             lap = (cs[t, pl.ds(base, 8), :] * (mid[t] - down[t])
                    - cs[t, pl.ds(base - 1, 8), :] * (up[t] - mid[t]))
-            out = ((v[1][t] + e0[t]) + (w2_[t] + flux[t])) + lap
-            q0[t, pl.ds(base, 8), :] = out
+            out.append(((v[1][t] + e0[t]) + (w2_[t] + flux[t])) + lap)
+        return out, mid
+
+    zero = jnp.zeros((8, 128), F32)
+
+    def apply0(i, carry):
+        gam, dad = carry
+        base = pl.multiple_of(i * 8 + 16, 8)
+        out, mid = apply_rows(d0, base, 9)
+        q0[8, pl.ds(base, 8), :] = out[8]
+        for t in range(8):
+            q0[t, pl.ds(base, 8), :] = out[t]
             gam = gam + r0[t, pl.ds(base, 8), :] * mid[t]
-            dad = dad + mid[t] * out
+            dad = dad + mid[t] * out[t]
         return gam, dad
 
     gam, dad = lax.fori_loop(0, 32, apply0, (zero, zero), unroll=4)
@@ -475,89 +483,125 @@
     b2 = cells * ctab[5, 0, 8:40, :]
     ctab[0, 0, 8:40, :] = b2
 
-    def q_tile(start, n):
-        lanes = lax.broadcasted_iota(jnp.int32, (n, 128), 1)
-        rows = pl.ds(start, n)
-        return jnp.where(lanes < 64, q0[0, rows, :], q0[7, rows, :])
-
-    tt2[0] = q_tile(16, 128).T
-    tt2[1] = q_tile(144, 128).T
+    sn2[...] = b2
     tbuf[0:8, :] = b2[24:32]
     tbuf[8:40, :] = b2
     tbuf[40:48, :] = b2[0:8]
-    tbuf[64:72, :] = q_tile(264, 8)
-    tbuf[72:80, :] = q_tile(16, 8)
-    tt2[2] = tbuf[...].T
-    for t in range(8):
-        sn2[t] = q0[t, 16:24, :]
-        ss2[t] = q0[t, 264:272, :]
-    sn2[8] = b2[0:8]
-    ss2[8] = b2[24:32]
-    copies2 = [(0, sn2, rs2), (1, ss2, rn2)] + side_copies(tt2, rx2, third)
+    tt2[0] = tbuf[...].T
+    copies2 = [(0, 0, sn2.at[pl.ds(0, 8), :], rs2), (1, 1, sn2.at[pl.ds(24, 8), :], rn2)]
+    copies2 += side_copies(tt2, rx2, pl.ds(0, 1), 8)
     start_all(2, copies2)
-    wait_recv_all(2, copies2)
-
-    unpack_fine(rx2)
-    for g in range(2):
-        q0[8, 16 + 128 * g:144 + 128 * g, :] = hbuf[g].T
-    tile = hbuf[2].T
-    q0[8, 8:16, :] = tile[64:72]
-    q0[8, 272:280, :] = tile[72:80]
-    ctab[0, 1, :, :] = tile[0:48]
-    for t in range(8):
-        q0[t, 8:16, :] = rn2[t]
-        q0[t, 272:280, :] = rs2[t]
-    ctab[0, 0, 0:8, :] = rn2[8]
-    ctab[0, 0, 40:48, :] = rs2[8]
-    jacobi()
-    precond(q0, w)
-
-    def blur1_rim(base):
+
+    def apply0_rim(i, _):
+        base = pl.multiple_of(i * 264 + 8, 8)
+        out, _ = apply_rows(d0, base, 9)
+        for t in range(9):
+            q0[t, pl.ds(base, 8), :] = out[t]
+        return 0
+
+    lax.fori_loop(0, 2, apply0_rim, 0, unroll=2)
+
+    def scaled(i, _):
+        here = pl.ds(pl.multiple_of(i * 8 + 8, 8), 8)
+        for t in range(9):
+            w[t, here, :] = q0[t, here, :] * rfd[t, here, :]
+        return 0
+
+    lax.fori_loop(0, 34, scaled, 0, unroll=4)
+
+    def blur1(i, _):
+        base = pl.multiple_of(i * 8 + 8, 8)
         out, _, _, _ = blur_rows(w, base)
         for t in range(9):
             img[t, pl.ds(base, 8), :] = out[t]
-
-    def blur1(i, carry):
+        return 0
+
+    lax.fori_loop(0, 34, blur1, 0, unroll=4)
+    clear_outside(img)
+
+    def apply1(i, carry):
         qw, waw = carry
         base = pl.multiple_of(i * 8 + 16, 8)
-        out, up, mid, down = blur_rows(w, base)
-        east = sh_east(mid)
-        flux = [ce[t, pl.ds(base, 8), :] * (mid[t] - east[t]) for t in range(9)]
-        fw = sh_west(flux)
-        img[8, pl.ds(base, 8), :] = out[8]
-        for t in range(8):
-            lap = (cs[t, pl.ds(base, 8), :] * (mid[t] - down[t])
-                   - cs[t, pl.ds(base - 1, 8), :] * (up[t] - mid[t]))
-            lap = lap + (flux[t] - fw[t])
-            img[t, pl.ds(base, 8), :] = out[t]
-            lw[t, pl.ds(base, 8), :] = lap
+        out, mid = apply_rows(w, base, 8)
+        for t in range(8):
+            lw[t, pl.ds(base, 8), :] = out[t]
             qw = qw + q0[t, pl.ds(base, 8), :] * mid[t]
-            waw = waw + (out[t] * out[t] + mid[t] * lap)
+            waw = waw + mid[t] * out[t]
         return qw, waw
 
-    blur1_rim(8)
-    blur1_rim(272)
-    qw, waw = lax.fori_loop(0, 32, blur1, (zero, zero), unroll=4)
+    qw, waw = lax.fori_loop(0, 32, apply1, (zero, zero), unroll=4)
+    at_cells = exact_dot(
+        jnp.concatenate([row_sums(lw, t) for t in range(8)], axis=1), cmat[:, 0:128])
+
+    wait_recv_all(2, copies2)
+    for dc, rows in ((-1, slice(0, 8)), (1, slice(120, 128))):
+        hbuf[0, rows, :] = side(rx2, 0, dc, lane < 8, lane < 40)
+    ctab[0, 1, :, :] = hbuf[0].T[0:48]
+    ctab[0, 0, 0:8, :] = rn2[...]
+    ctab[0, 0, 40:48, :] = rs2[...]
+    jacobi()
+    spread()
+
+    z = zs[0, 16:48, :]
+    ze = jnp.where(lane32 == 127, pltpu.roll(zs[1, 16:48, :], 127, 1), pltpu.roll(z, 127, 1))
+    zw = jnp.where(lane32 == 0, pltpu.roll(zs[1, 16:48, :], 1, 1), pltpu.roll(z, 1, 1))
+    g = [ctab[f, 0, 8:40, :] for f in range(5)]
+    lap = (g[1] * (z - ze) + g[2] * (z - zw)) + (
+        g[3] * (z - zs[0, 15:47, :]) + g[4] * (z - zs[0, 17:49, :]))
+
+    def fold(x):
+        return (x[0:8] + x[8:16]) + (x[16:24] + x[24:32])
+
+    qw = qw + fold(cells * z)
+    waw = waw + fold(z * (2.0 * at_cells + ctab[5, 1, 8:40, :] * lap))
+
+    for n in range(6):
+        rows = slice(8 * n, 8 * n + 8)
+        mid = [zup[t, rows, :] for t in range(9)]
+        east, west = sh_east(mid), sh_west(mid)
+        for t in range(8):
+            zeast[t, rows, :] = east[t]
+            zwest[t, rows, :] = west[t]
+    ksums = [(kk[0][b] + kk[1][b]) + kk[2][b] for b in range(3)]
+
+    def lanes_conv(weights, parts):
+        return weights[0] * parts[0] + weights[1] * parts[1] + weights[2] * parts[2]
+
+    for n in range(4):
+        at, up, down = (slice(8 * n + o, 8 * n + o + 8) for o in (8, 7, 9))
+        for t in range(8):
+            here = [x[t, at, :] for x in (zwest, zup, zeast)]
+            north = [x[t, up, :] for x in (zwest, zup, zeast)]
+            south = [x[t, down, :] for x in (zwest, zup, zeast)]
+            mid = lanes_conv(ksums, here)
+            first = mid + lanes_conv(kk[0], [p - q for p, q in zip(north, here)])
+            last = mid + lanes_conv(kk[2], [p - q for p, q in zip(south, here)])
+            waw = waw + (6.0 * (mid * mid) + (first * first + last * last))
 
     for n, part in enumerate((gam, dad, qw, waw)):
         red0[n:n + 1, :] = jnp.sum(part, axis=0, keepdims=True)
     red0[4:8, :] = jnp.zeros((4, 128), F32)
     redx[k8] = red0[...]
-    for i in range(zk):
-        @pl.when(k8 != i)
-        def _():
-            pltpu.make_async_remote_copy(
-                red0, redx.at[k8], rsend.at[0], rrecv.at[0],
-                device_id=zk_group[i], device_id_type=MESH).start()
+    for peer in zk_group:
+        pltpu.make_async_remote_copy(
+            red0, redx.at[k8], rsend.at[0], rrecv.at[0],
+            device_id=peer, device_id_type=MESH).start()
+
+    def add_coarse(i, _):
+        here = pl.ds(pl.multiple_of(i * 8 + 8, 8), 8)
+        for t in range(9):
+            w[t, here, :] = w[t, here, :] + zup[t, pl.ds(i + 7, 1), :]
+        return 0
+
+    lax.fori_loop(0, 34, add_coarse, 0, unroll=4)
+    lax.fori_loop(0, 34, blur1, 0, unroll=4)
     clear_outside(img)
 
-    def apply1(i, _):
+    def apply2(i, _):
         base = pl.multiple_of(i * 8 + 16, 8)
-        v = adjoint_parts(base)
-        e0, w2_ = sh_east(v[0]), sh_west(v[2])
-        for t in range(8):
-            here = pl.ds(base, 8)
-            lw[t, here, :] = ((v[1][t] + e0[t]) + w2_[t]) + lw[t, here, :]
+        out, _ = apply_rows(w, base, 8)
+        for t in range(8):
+            lw[t, pl.ds(base, 8), :] = out[t]
         return 0
 
     def all_bytes(buf, n, sem):
@@ -569,13 +613,15 @@
         total = total + redx[i]
     red1[...] = total
     redy[xy_me] = total
-    for i in range(n_rows * ny):
-        @pl.when(xy_me != i)
-        def _():
-            pltpu.make_async_remote_copy(
-                red1, redy.at[xy_me], rsend.at[1], rrecv.at[1],
-                device_id=xy_group[i], device_id_type=MESH).start()
-    lax.fori_loop(0, 32, apply1, 0, unroll=4)
+    for peer in xy_group:
+        pltpu.make_async_remote_copy(
+            red1, redy.at[xy_me], rsend.at[1], rrecv.at[1],
+            device_id=peer, device_id_type=MESH).start()
+    lax.fori_loop(0, 32, apply2, 0, unroll=4)
+    wait_send_all(0, copies0)
+    wait_send_all(1, copies1)
+    wait_send_all(2, copies2)
+    all_bytes(redx, zk - 1, rsend.at[0]).wait()
     all_bytes(redy, n_rows * ny - 1, rrecv.at[1]).wait()
     total = redy[0]
     for i in range(1, n_rows * ny):
@@ -595,28 +641,27 @@
 
     coef[0] = ca
     coef[1] = cb
-    wait_send_all(0, copies0)
-    wait_send_all(1, copies1)
-    wait_send_all(2, copies2)
-    all_bytes(redx, zk - 1, rsend.at[0]).wait()
     all_bytes(redy, n_rows * ny - 1, rsend.at[1]).wait()
 
 
 def finish_kernel(r0, d0, q0, w, lw, coef, sol_hbm, res_hbm, sol, res, out_sem):
     ca, cb = coef[0], coef[1]
     stores = []
-    for t in range(8):
+    for n in range(8):
         def finish(i, _):
-            src_rows = pl.ds(pl.multiple_of(i * 8 + 16, 8), 8)
-            dst_rows = pl.ds(pl.multiple_of(i * 8, 8), 8)
-            sol[t, dst_rows, :] = ca * d0[t, src_rows, :] - cb * w[t, src_rows, :]
-            res[t, dst_rows, :] = (r0[t, src_rows, :] - ca * q0[t, src_rows, :]) + cb * lw[t, src_rows, :]
+            dst_rows = pl.ds(pl.multiple_of(i * 8 + n * 32, 8), 8)
+            src_rows = pl.ds(pl.multiple_of(i * 8 + n * 32 + 16, 8), 8)
+            for t in range(8):
+                lanes = slice(t * 128, t * 128 + 128)
+                sol[dst_rows, lanes] = ca * d0[t, src_rows, :] - cb * w[t, src_rows, :]
+                res[dst_rows, lanes] = (
+                    r0[t, src_rows, :] - ca * q0[t, src_rows, :]) + cb * lw[t, src_rows, :]
             return 0
 
-        lax.fori_loop(0, 32, finish, 0, unroll=8)
-        lanes = pl.ds(t * 128, 128)
-        stores.append(pltpu.make_async_copy(sol.at[t], sol_hbm.at[:, lanes], out_sem.at[t]))
-        stores.append(pltpu.make_async_copy(res.at[t], res_hbm.at[:, lanes], out_sem.at[8 + t]))
+        lax.fori_loop(0, 4, finish, 0, unroll=2)
+        rows = pl.ds(n * 32, 32)
+        stores.append(pltpu.make_async_copy(sol.at[rows], sol_hbm.at[rows], out_sem.at[n]))
+        stores.append(pltpu.make_async_copy(res.at[rows], res_hbm.at[rows], out_sem.at[8 + n]))
         stores[-2].start()
         stores[-1].start()
     for x in stores:
@@ -627,7 +672,7 @@
     zk = min(8, n_cols)
     ny = n_cols // zk
     big = pltpu.VMEM((9, 288, 128), F32)
-    half = pltpu.VMEM((8, 256, 128), F32)
+    half = pltpu.VMEM((256, 1024), F32)
 
     def v(*shape):
         return pltpu.VMEM(shape, F32)
@@ -635,14 +680,13 @@
     scratch = [
         big, pltpu.VMEM((8, 256, 128), jnp.int32), big, big, big, big, big,
         v(9, 48, 128), pltpu.VMEM((1024, 256), BF16), pltpu.VMEM((128, 1152), BF16),
-        v(128, 128), v(3, 128, 128), v(3, 128, 128), v(3, 128, 128), v(3, 128, 128),
+        v(128, 128), v(3, 128, 128), v(3, 128, 128), v(1, 128, 128), v(3, 128, 128),
         v(6, 2, 48, 128), v(2, 64, 128),
-        v(8, 8, 128), v(8, 8, 128), v(8, 8, 128), v(8, 8, 128), v(8, 3, 8, 128),
-        v(5, 32, 128), v(5, 8, 128), v(5, 8, 128), v(8, 3, 8, 128),
-        v(9, 8, 128), v(9, 8, 128), v(9, 8, 128), v(9, 8, 128), v(8, 3, 8, 128),
+        v(8, 3, 16, 128), v(5, 32, 128), v(5, 8, 128), v(5, 8, 128), v(8, 3, 8, 128),
+        v(32, 128), v(8, 128), v(8, 128), v(8, 1, 8, 128), v(8, 48, 128), v(8, 48, 128),
         v(8, 128), v(8, 128), v(zk, 8, 128), v(n_rows * ny, 8, 128),
         pltpu.SemaphoreType.DMA((16,)),
-        pltpu.SemaphoreType.DMA((3, 8)), pltpu.SemaphoreType.DMA((3, 8)),
+        pltpu.SemaphoreType.DMA((3, 10)), pltpu.SemaphoreType.DMA((3, 10)),
         pltpu.SemaphoreType.DMA((2,)), pltpu.SemaphoreType.DMA((2,)),
     ]
     hbm = pl.BlockSpec(memory_space=pltpu.HBM)

time: 42.1 us -> 39.5 us (0.938)
  Pallas kernels: 41.3 us -> 38.7 us
    pallas_call x1, Pallas kernels: 39.8 us -> 37.2 us  [body(): pl.pallas_call(functools.partial(kernel, n_rows, n_cols, zk), out_shape=(...]
where the time goes in v3:
time: 39.5 us; the launch traced here: 39.3 us
  Pallas kernels  38.7 us (98%)
  between operations  0.64 us (2%)
    pallas_call x1, Pallas kernels, body(): pl.pallas_call(functools.partial(kernel, n_rows, n_cols, zk), out_shape=(...  37.2 us
    pallas_call x1, Pallas kernels, body(): pl.pallas_call(finish_kernel, out_shape=(shape, shape), in_specs=[vmem] *...  1.5 us

profile of v3, /device:TPU:1, one launch (start us, length us, event | category | flops | bytes accessed | tf_op | source)
XLA Modules:
  0.0 39.3 jit_solution(6830723047191976666)
XLA Ops:
  0.6 37.2 %shard_map.59 = (f32[9,288,128]{2,1,0:T(8,128)S(1)}, f32[9,288,128]{2,1,0:T(8,128)S(1)}, f32[9,288,128]{2,1,0:T(8,128)S(1)}, f32[9,288,128]{2,1,0:T(8,128)S(1)},...) custom-call(f32[4]{0:T(128)} %cw.1, f32[3,3]{1,0:T(4,128)} %bk.1, f32[256,1024]{1,0:T(8,128)} %obs_hbm.1, ...), custom_call_target="tpu_custom_call" | custom-call | tf_op jit(solution)/shard_map/pallas_call | solution.py:696
  37.8 1.5 %shard_map.60 = (f32[256,1024]{1,0:T(8,128)}, f32[256,1024]{1,0:T(8,128)}) custom-call(f32[9,288,128]{2,1,0:T(8,128)S(1)} %get-tuple-element.8.r0, f32[9,288,128]{2,1,0:T(8,128)S(1)} %get-tuple-element.9.d0, f32[9,288,128]{2,1,0:T(8,128)S(1)} %get-tuple-element.10.q0, f32[9,288,128]{2,1,0:T(8,128)S(1)} %get-tuple-element.11.w, ...), custom_call_target="tpu_custom_call" | custom-call | tf_op jit(solution)/shard_map/pallas_call | solution.py:706

commit v4 on v3

--- a/solution.py
+++ b/solution.py
@@ -28,8 +28,8 @@
     n_rows, n_cols, zk,
     cw, bk, obs_hbm, cls_hbm, r0, d0, q0, w, lw, coef,
     obs, cls, cond, rfd, ce, cs, img,
-    zup, cmat, umat, tbuf, tt0, tt1, tt2, hbuf, ctab, zs,
-    rx0, sn1, rn1, rs1, rx1, sn2, rn2, rs2, rx2, zeast, zwest,
+    zup, cmat, bmat, umat, tbuf, tt0, tt2, hbuf, ctab, zs,
+    rx0, sn1, sd1, rn1, rs1, rx1, pbuf, craw, sn2, rn2, rs2, rx2, zeast, zwest,
     red0, red1, redx, redy,
     in_sem, send_sem, recv_sem, rsend, rrecv,
 ):
@@ -55,6 +55,8 @@
 
     for buf in (rx0, rn1, rs1, rx1, rn2, rs2, rx2, hbuf, zs):
         buf[...] = jnp.zeros(buf.shape, F32)
+    pbuf[:, :, 0:16, :] = jnp.zeros((3, 8, 16, 128), F32)
+    pbuf[:, :, 48:64, :] = jnp.zeros((3, 8, 16, 128), F32)
     for buf in (obs, cond):
         for t in range(8):
             buf[t, 8:16, :] = jnp.zeros((8, 128), F32)
@@ -196,8 +198,11 @@
 
     ii = lax.broadcasted_iota(jnp.int32, (1024, 128), 0)
     jj = lax.broadcasted_iota(jnp.int32, (1024, 128), 1)
-    cmat[:, 0:128] = jnp.where(ii // 8 == jj, 1.0, 0.0).astype(BF16)
-    cmat[:, 128:256] = jnp.where(ii == jj * 8 + 7, 1.0, 0.0).astype(BF16)
+    for n, hit in enumerate((ii // 8 == jj, ii == jj * 8 + 7, ii == jj * 8)):
+        cmat[:, 128 * n:128 * n + 128] = jnp.where(hit, 1.0, 0.0).astype(BF16)
+    for b in range(3):
+        hit = (ii + 7 + b) // 8 == jj + 1
+        bmat[1024 * b:1024 * b + 1024, :] = jnp.where(hit, 1.0, 0.0).astype(BF16)
     ui = lax.broadcasted_iota(jnp.int32, (128, 1024), 0)
     uj = lax.broadcasted_iota(jnp.int32, (128, 1024), 1)
     umat[:, 0:1024] = jnp.where(uj // 8 == ui, 1.0, 0.0).astype(BF16)
@@ -205,6 +210,81 @@
     vj = lax.broadcasted_iota(jnp.int32, (128, 128), 1)
     umat[:, 1024:1152] = jnp.where(
         ((vj < 64) & (vi == 0)) | ((vj >= 64) & (vi == 127)), 1.0, 0.0).astype(BF16)
+
+    def row_sums(ref, t):
+        total = ref[t, pl.ds(16, 32, stride=8), :]
+        for s in range(1, 8):
+            total = total + ref[t, pl.ds(16 + s, 32, stride=8), :]
+        return total
+
+    lane32 = lax.broadcasted_iota(jnp.int32, (32, 128), 1)
+    row32 = lax.broadcasted_iota(jnp.int32, (32, 128), 0)
+    lane48 = lax.broadcasted_iota(jnp.int32, (48, 128), 1)
+    row48 = lax.broadcasted_iota(jnp.int32, (48, 128), 0)
+    last48, first48 = lane48 == 127, lane48 == 0
+
+    every = pl.ds(16, 32, stride=8)
+    last_row = pl.ds(23, 32, stride=8)
+    sums = exact_dot(jnp.concatenate([
+        jnp.concatenate([row_sums(cond, t) for t in range(8)], axis=1),
+        jnp.concatenate([cond[t, every, :] for t in range(8)], axis=1),
+        jnp.concatenate([cond[t, last_row, :] for t in range(8)], axis=1)], axis=0), cmat[...])
+    ec, wc = sums[0:32, 128:256], sums[0:32, 256:384]
+    nc, sc = sums[32:64, 0:128], sums[64:96, 0:128]
+    part = (
+        0.5 * (ec + jnp.where(lane32 == 127, 0.0, pltpu.roll(wc, 127, 1))),
+        0.5 * (wc + jnp.where(lane32 == 0, 0.0, pltpu.roll(ec, 1, 1))),
+        0.5 * (nc + jnp.where(row32 == 0, 0.0, pltpu.roll(sc, 1, 0))),
+        0.5 * (sc + jnp.where(row32 == 31, 0.0, pltpu.roll(nc, 31, 0))),
+    )
+
+    for t in range(8):
+        pbuf[0, t, 16:48, :] = row_sums(obs, t)
+        pbuf[1, t, 16:48, :] = obs[t, every, :]
+        pbuf[2, t, 16:48, :] = obs[t, last_row, :]
+    vb = [[], [], []]
+    for t in range(8):
+        mid = pbuf[0, t, 8:56, :]
+        down = mid - pbuf[1, t, 8:56, :] + pbuf[1, t, 9:57, :]
+        up = mid - pbuf[2, t, 8:56, :] + pbuf[2, t, 7:55, :]
+        for b in range(3):
+            vb[b].append(kk[0][b] * down + kk[1][b] * mid + kk[2][b] * up)
+    own_source = exact_dot(jnp.concatenate(vb[0] + vb[1] + vb[2], axis=1), bmat[...])
+    own_ring = jnp.where(lane48 == 7, pltpu.roll(vb[0][0], 7, 1),
+                         jnp.where(lane48 == 8, pltpu.roll(vb[2][7], 9, 1), 0.0))
+
+    for f in range(4):
+        sn1[0, f] = part[f][0:8]
+        sn1[1, f] = part[f][24:32]
+        craw[f, 0, 8:40, :] = part[f]
+    for h in range(2):
+        sn1[0, 4 + h] = own_source[8 * h:8 * h + 8]
+        sn1[0, 6 + h] = own_ring[8 * h:8 * h + 8]
+        sn1[1, 4 + h] = own_source[32 + 8 * h:40 + 8 * h]
+        sn1[1, 6 + h] = own_ring[32 + 8 * h:40 + 8 * h]
+    for g in range(2):
+        for h in range(2):
+            field = part[2 * g + h]
+            tbuf[64 * h:64 * h + 8, :] = field[24:32]
+            tbuf[64 * h + 8:64 * h + 40, :] = field
+            tbuf[64 * h + 40:64 * h + 48, :] = field[0:8]
+        tile = tbuf[...].T
+        sd1[0, g] = tile[0:8]
+        sd1[1, g] = tile[120:128]
+    tbuf[0:48, :] = own_source
+    tbuf[64:112, :] = own_ring
+    tile = tbuf[...].T
+    in48 = lane < 48
+    sd1[0, 2] = jnp.where(in48, pltpu.roll(tile[0:8], 64, 1), 0.0)
+    sd1[0, 3] = jnp.where(in48, tile[0:8], 0.0)
+    sd1[1, 2] = jnp.where(in48, tile[120:128], 0.0)
+    sd1[1, 3] = jnp.where(in48, pltpu.roll(tile[8:16], 64, 1), 0.0)
+
+    copies1 = [(0, 0, sn1.at[0], rs1), (1, 1, sn1.at[1], rn1)]
+    for n, (dr, dc) in enumerate(NB):
+        if dc:
+            copies1.append((n, n, sd1.at[0 if dc < 0 else 1], rx1.at[n]))
+    start_all(1, copies1)
 
     def blur_adjoint(up, mid, down, b):
         return kk[0][b] * down + kk[1][b] * mid + kk[2][b] * up
@@ -314,50 +394,6 @@
         def _():
             ref[8, 8:280, :] = jnp.where(lanes >= 64, ref[8, 8:280, :], 0.0)
 
-    def row_sums(ref, t):
-        total = ref[t, pl.ds(16, 32, stride=8), :]
-        for s in range(1, 8):
-            total = total + ref[t, pl.ds(16 + s, 32, stride=8), :]
-        return total
-
-    src = jnp.concatenate([row_sums(r0, t) for t in range(8)], axis=1)
-    esum = jnp.concatenate([row_sums(ce, t) for t in range(8)], axis=1)
-    srow = jnp.concatenate([cs[t, pl.ds(23, 32, stride=8), :] for t in range(8)], axis=1)
-    nrow = jnp.concatenate([cs[t, 8:16, :] for t in range(8)], axis=1)
-    stack = jnp.concatenate([src, esum, srow, nrow], axis=0)
-    sums = exact_dot(stack, cmat[...])
-    source = sums[0:32, 0:128]
-    c_east = sums[32:64, 128:256]
-    c_south = sums[64:96, 0:128]
-    outer = row_sums(ce, 8)
-    lane32 = lax.broadcasted_iota(jnp.int32, (32, 128), 1)
-    c_west = jnp.where(lane32 == 0, pltpu.roll(outer, 1, 1), pltpu.roll(c_east, 1, 1))
-    zs[0, 0:8, :] = sums[96:104, 0:128]
-    zs[0, 8:40, :] = c_south
-    c_north = zs[0, 7:39, :]
-    zs[...] = jnp.zeros(zs.shape, F32)
-    c_diag = 64.0 * (ksum * ksum) + c_east + c_west + c_north + c_south
-    scale = OMEGA / c_diag
-    fields = (source * scale, c_east * scale, c_west * scale, c_north * scale, c_south * scale)
-    ctab[5, 0, 8:40, :] = scale
-    ctab[5, 1, 8:40, :] = c_diag * (1.0 / OMEGA)
-    for f in range(5):
-        ctab[f, 0, 8:40, :] = fields[f]
-        sn1[f] = fields[f]
-    for g in range(3):
-        for h in range(2):
-            f = 2 * g + h
-            if f < 5:
-                tbuf[64 * h:64 * h + 8, :] = fields[f][24:32]
-                tbuf[64 * h + 8:64 * h + 40, :] = fields[f]
-                tbuf[64 * h + 40:64 * h + 48, :] = fields[f][0:8]
-        tt1[g] = tbuf[...].T
-
-    whole = pl.ds(0, 3)
-    copies1 = [(0, 0, sn1.at[:, pl.ds(0, 8), :], rs1), (1, 1, sn1.at[:, pl.ds(24, 8), :], rn1)]
-    copies1 += side_copies(tt1, rx1, whole, 8)
-    start_all(1, copies1)
-
     def diag_body(i, _):
         base = pl.multiple_of(i * 8 + 8, 8)
         here = pl.ds(base, 8)
@@ -372,22 +408,55 @@
     clear_outside(rfd)
     wait_recv_all(1, copies1)
 
-    for f in range(5):
-        ctab[f, 0, 0:8, :] = rn1[f]
-        ctab[f, 0, 40:48, :] = rs1[f]
+    for f in range(4):
+        craw[f, 0, 0:8, :] = rn1[f]
+        craw[f, 0, 40:48, :] = rs1[f]
     hbuf[:, 8:16, :] = jnp.zeros((3, 8, 128), F32)
     hbuf[:, 112:120, :] = jnp.zeros((3, 8, 128), F32)
-    for g in range(3):
+    for g in range(2):
         for dc, rows in ((-1, slice(0, 8)), (1, slice(120, 128))):
             hbuf[g, rows, :] = side(rx1, g, dc, lane64 < 8, lane64 < 40)
         tile = hbuf[g].T
         for h in range(2):
-            f = 2 * g + h
-            if f < 5:
-                ctab[f, 1, :, :] = tile[64 * h:64 * h + 48]
-
-    lane48 = lax.broadcasted_iota(jnp.int32, (48, 128), 1)
-    last48, first48 = lane48 == 127, lane48 == 0
+            craw[2 * g + h, 1] = tile[64 * h:64 * h + 48]
+    for dc, blocks in ((-1, ((2, slice(8, 16)), (3, slice(0, 8)))),
+                       (1, ((2, slice(120, 128)), (3, slice(112, 120))))):
+        for q, rows in blocks:
+            hbuf[2, rows, :] = rx1[NB.index((0, dc)), q] + (
+                pltpu.roll(rx1[NB.index((1, dc)), q], 96, 1)
+                + pltpu.roll(rx1[NB.index((-1, dc)), q], 32, 1))
+    tile = hbuf[2].T[0:48]
+    blank = jnp.zeros((16, 128), F32)
+
+    def with_rows(own_part, q):
+        return own_part + jnp.concatenate(
+            [rn1[q], rn1[q + 1], blank, rs1[q], rs1[q + 1]], axis=0)
+
+    ring_all = pltpu.roll(with_rows(own_ring, 6), 120, 1)
+    source = [
+        with_rows(own_source, 4) + jnp.where(
+            last48, pltpu.roll(tile, 112, 1), jnp.where(first48, pltpu.roll(tile, 16, 1), 0.0)),
+        tile + jnp.where(last48 | first48, ring_all, 0.0),
+    ]
+    for t in range(2):
+        for a, b in ((7, 8), (39, 40)):
+            both = craw[3, t, a:a + 1, :] + craw[2, t, b:b + 1, :]
+            craw[3, t, a:a + 1, :] = both
+            craw[2, t, b:b + 1, :] = both
+    pe, pw = [craw[0, t] for t in range(2)], [craw[1, t] for t in range(2)]
+    rows_ok = ((row48 >= 8) | (r > 0)) & ((row48 < 40) | (r < n_rows - 1))
+    lanes_ok = ((lane48 >= 64) | (c < n_cols - 1)) & ((lane48 < 64) | (c > 0))
+    for t in range(2):
+        c_east = pe[t] + jnp.where(last48, pltpu.roll(pw[1 - t], 127, 1), 0.0)
+        c_west = pw[t] + jnp.where(first48, pltpu.roll(pe[1 - t], 1, 1), 0.0)
+        c_north, c_south = craw[2, t], craw[3, t]
+        c_diag = 64.0 * (ksum * ksum) + c_east + c_west + c_north + c_south
+        scale = jnp.where(rows_ok & lanes_ok if t else rows_ok, OMEGA / c_diag, 0.0)
+        for f, x in enumerate((source[t], c_east, c_west, c_north, c_south)):
+            ctab[f, t] = x * scale
+        if t == 0:
+            ctab[5, 0] = scale
+            ctab[5, 1] = c_diag * (1.0 / OMEGA)
 
     def sweep(_, carry):
         z = [zs[t, 8:56, :] for t in range(2)]
@@ -679,10 +748,12 @@
 
     scratch = [
         big, pltpu.VMEM((8, 256, 128), jnp.int32), big, big, big, big, big,
-        v(9, 48, 128), pltpu.VMEM((1024, 256), BF16), pltpu.VMEM((128, 1152), BF16),
-        v(128, 128), v(3, 128, 128), v(3, 128, 128), v(1, 128, 128), v(3, 128, 128),
+        v(9, 48, 128), pltpu.VMEM((1024, 384), BF16), pltpu.VMEM((3072, 128), BF16),
+        pltpu.VMEM((128, 1152), BF16),
+        v(128, 128), v(3, 128, 128), v(1, 128, 128), v(3, 128, 128),
         v(6, 2, 48, 128), v(2, 64, 128),
-        v(8, 3, 16, 128), v(5, 32, 128), v(5, 8, 128), v(5, 8, 128), v(8, 3, 8, 128),
+        v(8, 3, 16, 128), v(2, 8, 8, 128), v(2, 4, 8, 128), v(8, 8, 128), v(8, 8, 128),
+        v(8, 4, 8, 128), v(3, 8, 64, 128), v(4, 2, 48, 128),
         v(32, 128), v(8, 128), v(8, 128), v(8, 1, 8, 128), v(8, 48, 128), v(8, 48, 128),
         v(8, 128), v(8, 128), v(zk, 8, 128), v(n_rows * ny, 8, 128),
         pltpu.SemaphoreType.DMA((16,)),

time: 39.5 us -> 36.8 us (0.932)
  Pallas kernels: 38.7 us -> 36 us
    pallas_call x1, Pallas kernels: 37.2 us -> 34.5 us  [body(): pl.pallas_call(functools.partial(kernel, n_rows, n_cols, zk), out_shape=(...]
where the time goes in v4:
time: 36.8 us; the launch traced here: 36.6 us
  Pallas kernels  36 us (98%)
  between operations  0.64 us (2%)
    pallas_call x1, Pallas kernels, body(): pl.pallas_call(functools.partial(kernel, n_rows, n_cols, zk), out_shape=(...  34.5 us
    pallas_call x1, Pallas kernels, body(): pl.pallas_call(finish_kernel, out_shape=(shape, shape), in_specs=[vmem] *...  1.5 us

profile of v4, /device:TPU:1, one launch (start us, length us, event | category | flops | bytes accessed | tf_op | source)
XLA Modules:
  0.0 36.6 jit_solution(1993634515271363031)
XLA Ops:
  0.6 34.5 %shard_map.59 = (f32[9,288,128]{2,1,0:T(8,128)S(1)}, f32[9,288,128]{2,1,0:T(8,128)S(1)}, f32[9,288,128]{2,1,0:T(8,128)S(1)}, f32[9,288,128]{2,1,0:T(8,128)S(1)},...) custom-call(f32[4]{0:T(128)} %cw.1, f32[3,3]{1,0:T(4,128)} %bk.1, f32[256,1024]{1,0:T(8,128)} %obs_hbm.1, ...), custom_call_target="tpu_custom_call" | custom-call | tf_op jit(solution)/shard_map/pallas_call | solution.py:767
  35.1 1.5 %shard_map.60 = (f32[256,1024]{1,0:T(8,128)}, f32[256,1024]{1,0:T(8,128)}) custom-call(f32[9,288,128]{2,1,0:T(8,128)S(1)} %get-tuple-element.8.r0, f32[9,288,128]{2,1,0:T(8,128)S(1)} %get-tuple-element.9.d0, f32[9,288,128]{2,1,0:T(8,128)S(1)} %get-tuple-element.10.q0, f32[9,288,128]{2,1,0:T(8,128)S(1)} %get-tuple-element.11.w, ...), custom_call_target="tpu_custom_call" | custom-call | tf_op jit(solution)/shard_map/pallas_call | solution.py:777

commit v5 on v4

--- a/solution.py
+++ b/solution.py
@@ -55,8 +55,6 @@
 
     for buf in (rx0, rn1, rs1, rx1, rn2, rs2, rx2, hbuf, zs):
         buf[...] = jnp.zeros(buf.shape, F32)
-    pbuf[:, :, 0:16, :] = jnp.zeros((3, 8, 16, 128), F32)
-    pbuf[:, :, 48:64, :] = jnp.zeros((3, 8, 16, 128), F32)
     for buf in (obs, cond):
         for t in range(8):
             buf[t, 8:16, :] = jnp.zeros((8, 128), F32)
@@ -117,6 +115,15 @@
 
     def rows_of(ref, base, n=9):
         return [ref[t, pl.ds(base, 8), :] for t in range(n)]
+
+    ii = lax.broadcasted_iota(jnp.int32, (1024, 128), 0)
+    jj = lax.broadcasted_iota(jnp.int32, (1024, 128), 1)
+    cell, place = jnp.right_shift(ii, 3), jnp.bitwise_and(ii, 7)
+    for n, hit in enumerate((cell == jj, (cell == jj) & (place == 7), (cell == jj) & (place == 0))):
+        cmat[:, 128 * n:128 * n + 128] = jnp.where(hit, 1.0, 0.0).astype(BF16)
+    for b in range(3):
+        hit = jnp.right_shift(ii + (7 + b), 3) == jj + 1
+        bmat[1024 * b:1024 * b + 1024, :] = jnp.where(hit, 1.0, 0.0).astype(BF16)
 
     for x in loads:
         x.wait()
@@ -195,21 +202,6 @@
         copies0.append((q + 1, 1, field.at[own, low, :], field.at[own, above, :]))
     pl.semaphore_wait(bar, peers)
     start_all(0, copies0)
-
-    ii = lax.broadcasted_iota(jnp.int32, (1024, 128), 0)
-    jj = lax.broadcasted_iota(jnp.int32, (1024, 128), 1)
-    for n, hit in enumerate((ii // 8 == jj, ii == jj * 8 + 7, ii == jj * 8)):
-        cmat[:, 128 * n:128 * n + 128] = jnp.where(hit, 1.0, 0.0).astype(BF16)
-    for b in range(3):
-        hit = (ii + 7 + b) // 8 == jj + 1
-        bmat[1024 * b:1024 * b + 1024, :] = jnp.where(hit, 1.0, 0.0).astype(BF16)
-    ui = lax.broadcasted_iota(jnp.int32, (128, 1024), 0)
-    uj = lax.broadcasted_iota(jnp.int32, (128, 1024), 1)
-    umat[:, 0:1024] = jnp.where(uj // 8 == ui, 1.0, 0.0).astype(BF16)
-    vi = lax.broadcasted_iota(jnp.int32, (128, 128), 0)
-    vj = lax.broadcasted_iota(jnp.int32, (128, 128), 1)
-    umat[:, 1024:1152] = jnp.where(
-        ((vj < 64) & (vi == 0)) | ((vj >= 64) & (vi == 127)), 1.0, 0.0).astype(BF16)
 
     def row_sums(ref, t):
         total = ref[t, pl.ds(16, 32, stride=8), :]
@@ -238,6 +230,8 @@
         0.5 * (sc + jnp.where(row32 == 31, 0.0, pltpu.roll(nc, 31, 0))),
     )
 
+    pbuf[:, :, 0:16, :] = jnp.zeros((3, 8, 16, 128), F32)
+    pbuf[:, :, 48:64, :] = jnp.zeros((3, 8, 16, 128), F32)
     for t in range(8):
         pbuf[0, t, 16:48, :] = row_sums(obs, t)
         pbuf[1, t, 16:48, :] = obs[t, every, :]
@@ -286,6 +280,14 @@
             copies1.append((n, n, sd1.at[0 if dc < 0 else 1], rx1.at[n]))
     start_all(1, copies1)
 
+    ui = lax.broadcasted_iota(jnp.int32, (128, 1024), 0)
+    uj = lax.broadcasted_iota(jnp.int32, (128, 1024), 1)
+    umat[:, 0:1024] = jnp.where(jnp.right_shift(uj, 3) == ui, 1.0, 0.0).astype(BF16)
+    vi = lax.broadcasted_iota(jnp.int32, (128, 128), 0)
+    vj = lax.broadcasted_iota(jnp.int32, (128, 128), 1)
+    umat[:, 1024:1152] = jnp.where(
+        ((vj < 64) & (vi == 0)) | ((vj >= 64) & (vi == 127)), 1.0, 0.0).astype(BF16)
+
     def blur_adjoint(up, mid, down, b):
         return kk[0][b] * down + kk[1][b] * mid + kk[2][b] * up
 
@@ -371,7 +373,7 @@
             cs[t, here, :] = 0.5 * (cm[t] + csouth[t])
         return 0
 
-    lax.fori_loop(0, 4, outer_body, 0, unroll=2)
+    lax.fori_loop(0, 4, outer_body, 0, unroll=4)
 
     def clear_outside(ref):
         @pl.when(r == 0)
@@ -477,7 +479,7 @@
     def jacobi():
         for t in range(2):
             zs[t, 8:56, :] = ctab[0, t]
-        lax.fori_loop(0, SWEEPS - 1, sweep, 0)
+        lax.fori_loop(0, SWEEPS - 1, sweep, 0, unroll=SWEEPS - 1)
 
     def spread():
         up = exact_dot(zs[0, 8:56, :], umat[:, 0:1024])

time: 36.8 us -> 36.4 us (0.989)
  Pallas kernels: 36 us -> 35.6 us
where the time goes in v5:
time: 36.4 us; the launch traced here: 36.3 us
  Pallas kernels  35.6 us (98%)
  between operations  0.64 us (2%)
    pallas_call x1, Pallas kernels, body(): pl.pallas_call(functools.partial(kernel, n_rows, n_cols, zk), out_shape=(...  34.1 us
    pallas_call x1, Pallas kernels, body(): pl.pallas_call(finish_kernel, out_shape=(shape, shape), in_specs=[vmem] *...  1.5 us

profile of v5, /device:TPU:1, one launch (start us, length us, event | category | flops | bytes accessed | tf_op | source)
XLA Modules:
  0.0 36.3 jit_solution(47965265588982066)
XLA Ops:
  0.6 34.1 %shard_map.59 = (f32[9,288,128]{2,1,0:T(8,128)S(1)}, f32[9,288,128]{2,1,0:T(8,128)S(1)}, f32[9,288,128]{2,1,0:T(8,128)S(1)}, f32[9,288,128]{2,1,0:T(8,128)S(1)},...) custom-call(f32[4]{0:T(128)} %cw.1, f32[3,3]{1,0:T(4,128)} %bk.1, f32[256,1024]{1,0:T(8,128)} %obs_hbm.1, ...), custom_call_target="tpu_custom_call" | custom-call | tf_op jit(solution)/shard_map/pallas_call | solution.py:769
  34.8 1.5 %shard_map.60 = (f32[256,1024]{1,0:T(8,128)}, f32[256,1024]{1,0:T(8,128)}) custom-call(f32[9,288,128]{2,1,0:T(8,128)S(1)} %get-tuple-element.8.r0, f32[9,288,128]{2,1,0:T(8,128)S(1)} %get-tuple-element.9.d0, f32[9,288,128]{2,1,0:T(8,128)S(1)} %get-tuple-element.10.q0, f32[9,288,128]{2,1,0:T(8,128)S(1)} %get-tuple-element.11.w, ...), custom_call_target="tpu_custom_call" | custom-call | tf_op jit(solution)/shard_map/pallas_call | solution.py:779

commit v6 on v5

--- a/solution.py
+++ b/solution.py
@@ -541,8 +541,10 @@
         base = pl.multiple_of(i * 8 + 16, 8)
         out, mid = apply_rows(d0, base, 9)
         q0[8, pl.ds(base, 8), :] = out[8]
+        w[8, pl.ds(base, 8), :] = out[8] * rfd[8, pl.ds(base, 8), :]
         for t in range(8):
             q0[t, pl.ds(base, 8), :] = out[t]
+            w[t, pl.ds(base, 8), :] = out[t] * rfd[t, pl.ds(base, 8), :]
             gam = gam + r0[t, pl.ds(base, 8), :] * mid[t]
             dad = dad + mid[t] * out[t]
         return gam, dad
@@ -568,17 +570,10 @@
         out, _ = apply_rows(d0, base, 9)
         for t in range(9):
             q0[t, pl.ds(base, 8), :] = out[t]
+            w[t, pl.ds(base, 8), :] = out[t] * rfd[t, pl.ds(base, 8), :]
         return 0
 
     lax.fori_loop(0, 2, apply0_rim, 0, unroll=2)
-
-    def scaled(i, _):
-        here = pl.ds(pl.multiple_of(i * 8 + 8, 8), 8)
-        for t in range(9):
-            w[t, here, :] = q0[t, here, :] * rfd[t, here, :]
-        return 0
-
-    lax.fori_loop(0, 34, scaled, 0, unroll=4)
 
     def blur1(i, _):
         base = pl.multiple_of(i * 8 + 8, 8)

time: 36.4 us -> 36.3 us (level)
  no operation moved by 1% of the time
where the time goes in v6:
time: 36.3 us; the launch traced here: 36.1 us
  Pallas kernels  35.5 us (98%)
  between operations  0.64 us (2%)
    pallas_call x1, Pallas kernels, body(): pl.pallas_call(functools.partial(kernel, n_rows, n_cols, zk), out_shape=(...  34 us
    pallas_call x1, Pallas kernels, body(): pl.pallas_call(finish_kernel, out_shape=(shape, shape), in_specs=[vmem] *...  1.5 us

profile of v6, /device:TPU:1, one launch (start us, length us, event | category | flops | bytes accessed | tf_op | source)
XLA Modules:
  0.0 36.1 jit_solution(5956804489803725760)
XLA Ops:
  0.6 34.0 %shard_map.59 = (f32[9,288,128]{2,1,0:T(8,128)S(1)}, f32[9,288,128]{2,1,0:T(8,128)S(1)}, f32[9,288,128]{2,1,0:T(8,128)S(1)}, f32[9,288,128]{2,1,0:T(8,128)S(1)},...) custom-call(f32[4]{0:T(128)} %cw.1, f32[3,3]{1,0:T(4,128)} %bk.1, f32[256,1024]{1,0:T(8,128)} %obs_hbm.1, ...), custom_call_target="tpu_custom_call" | custom-call | tf_op jit(solution)/shard_map/pallas_call | solution.py:764
  34.6 1.5 %shard_map.60 = (f32[256,1024]{1,0:T(8,128)}, f32[256,1024]{1,0:T(8,128)}) custom-call(f32[9,288,128]{2,1,0:T(8,128)S(1)} %get-tuple-element.8.r0, f32[9,288,128]{2,1,0:T(8,128)S(1)} %get-tuple-element.9.d0, f32[9,288,128]{2,1,0:T(8,128)S(1)} %get-tuple-element.10.q0, f32[9,288,128]{2,1,0:T(8,128)S(1)} %get-tuple-element.11.w, ...), custom_call_target="tpu_custom_call" | custom-call | tf_op jit(solution)/shard_map/pallas_call | solution.py:774

commit v7 on v6

--- a/solution.py
+++ b/solution.py
@@ -408,6 +408,14 @@
 
     lax.fori_loop(0, 34, diag_body, 0, unroll=4)
     clear_outside(rfd)
+
+    def scale_first(i, _):
+        here = pl.ds(pl.multiple_of(i * 8 + 8, 8), 8)
+        for t in range(9):
+            d0[t, here, :] = r0[t, here, :] * rfd[t, here, :]
+        return 0
+
+    lax.fori_loop(0, 34, scale_first, 0, unroll=4)
     wait_recv_all(1, copies1)
 
     for f in range(4):
@@ -490,17 +498,13 @@
     jacobi()
     spread()
 
-    def precond(field, out):
-        def body(i, _):
-            base = pl.multiple_of(i * 8 + 8, 8)
-            here = pl.ds(base, 8)
-            for t in range(9):
-                out[t, here, :] = field[t, here, :] * rfd[t, here, :] + zup[t, pl.ds(i + 7, 1), :]
-            return 0
-
-        lax.fori_loop(0, 34, body, 0, unroll=4)
-
-    precond(r0, d0)
+    def add_first(i, _):
+        here = pl.ds(pl.multiple_of(i * 8 + 8, 8), 8)
+        for t in range(9):
+            d0[t, here, :] = d0[t, here, :] + zup[t, pl.ds(i + 7, 1), :]
+        return 0
+
+    lax.fori_loop(0, 34, add_first, 0, unroll=4)
 
     def blur_rows(ref, base):
         up, mid, down = rows_of(ref, base - 1), rows_of(ref, base), rows_of(ref, base + 1)

time: 36.3 us -> 36.4 us (level)
  no operation moved by 1% of the time
where the time goes in v7:
time: 36.4 us; the launch traced here: 36.2 us
  Pallas kernels  35.6 us (98%)
  between operations  0.64 us (2%)
    pallas_call x1, Pallas kernels, body(): pl.pallas_call(functools.partial(kernel, n_rows, n_cols, zk), out_shape=(...  34.1 us
    pallas_call x1, Pallas kernels, body(): pl.pallas_call(finish_kernel, out_shape=(shape, shape), in_specs=[vmem] *...  1.5 us

profile of v7, /device:TPU:1, one launch (start us, length us, event | category | flops | bytes accessed | tf_op | source)
XLA Modules:
  0.0 36.2 jit_solution(3603769742040277235)
XLA Ops:
  0.6 34.1 %shard_map.59 = (f32[9,288,128]{2,1,0:T(8,128)S(1)}, f32[9,288,128]{2,1,0:T(8,128)S(1)}, f32[9,288,128]{2,1,0:T(8,128)S(1)}, f32[9,288,128]{2,1,0:T(8,128)S(1)},...) custom-call(f32[4]{0:T(128)} %cw.1, f32[3,3]{1,0:T(4,128)} %bk.1, f32[256,1024]{1,0:T(8,128)} %obs_hbm.1, ...), custom_call_target="tpu_custom_call" | custom-call | tf_op jit(solution)/shard_map/pallas_call | solution.py:768
  34.7 1.5 %shard_map.60 = (f32[256,1024]{1,0:T(8,128)}, f32[256,1024]{1,0:T(8,128)}) custom-call(f32[9,288,128]{2,1,0:T(8,128)S(1)} %get-tuple-element.8.r0, f32[9,288,128]{2,1,0:T(8,128)S(1)} %get-tuple-element.9.d0, f32[9,288,128]{2,1,0:T(8,128)S(1)} %get-tuple-element.10.q0, f32[9,288,128]{2,1,0:T(8,128)S(1)} %get-tuple-element.11.w, ...), custom_call_target="tpu_custom_call" | custom-call | tf_op jit(solution)/shard_map/pallas_call | solution.py:778
